TPU v7x, 128 devices: a whole 4x4x4 slice. The times are simulated.
128 devices in a mesh: expert: 32 (over x, z, core), tensor: 4 (over y).
Axes of the slice: x: 4, y: 4, z: 4, core: 2. Of those that a mesh axis runs over, the one named last changes fastest.
Arguments:
- query_nope: bfloat16 [1024, 16384], P('expert', 'tensor'), may hold values from -6 to 6
- query_rope: bfloat16 [1024, 8192], P('expert', 'tensor'), may hold values from -14 to 14
- key_absorb: bfloat16 [128, 128, 512], P('tensor'), may hold values from -0.5 to 0.5
- latent_cache: bfloat16 [1024, 512, 576], P(('expert', 'tensor')), may hold values from -4 to 4
- new_latent: bfloat16 [1024, 576], P(('expert', 'tensor')), may hold values from -6 to 6
- context_lengths: int32 [1024], P(('expert', 'tensor')), may hold values from 2 to 512
- value_absorb: bfloat16 [128, 512, 128], P('tensor'), may hold values from -0.25 to 0.25
- out_proj: bfloat16 [16384, 7168], P('tensor', 'expert'), may hold values from -0.1875 to 0.1875
- residual: bfloat16 [1024, 7168], P(('expert', 'tensor')), may hold values from -6 to 6
- norm_gain: bfloat16 [7168], replicated, may hold values from 0.099609375 to 1.8984375
- routes: int32 [1024, 8], P(('expert', 'tensor')), may hold values from 0 to 31, all different within a row; in each aligned block of 8 rows (0 to 7, 8 to 15, ...) at most 4 rows name the same one
- gate_weights: float32 [1024, 8], P(('expert', 'tensor')), may hold values from 0.1 to 1
- expert_gate: bfloat16 [32, 7168, 1024], P('expert', None, 'tensor'), may hold values from -0.0625 to 0.0625
- expert_up: bfloat16 [32, 7168, 1024], P('expert', None, 'tensor'), may hold values from -0.0625 to 0.0625
- expert_down: bfloat16 [32, 1024, 7168], P('expert', 'tensor'), may hold values from -0.1875 to 0.1875
Outputs:
- layer_out: bfloat16 [1024, 7168], P(('expert', 'tensor'))
Inputs may be any that keep to these rules, and one draw needn't show every extreme that they name: `routes`: in each aligned block of 8 rows (the rows of one device) no expert is named by more than 4 rows, a bound that some block reaches.
All inputs are finite; a program needn't handle non-finite values.
Results may differ from a plain program's by a relative error of at most 0.02.
Values may be sent and summed in bfloat16 or wider, within the bound.
A program may use at most 128 MiB of HBM per device.

v0:
```python
import math

import jax
import jax.numpy as jnp
from jax import lax
from jax.sharding import PartitionSpec as P


def per_device(
    query_nope,
    query_rope,
    key_absorb,
    latent_cache,
    new_latent,
    context_lengths,
    value_absorb,
    out_proj,
    residual,
    norm_gain,
    routes,
    gate_weights,
    expert_gate,
    expert_up,
    expert_down,
):
    expert_count = lax.axis_size("expert")
    tensor_count = lax.axis_size("tensor")
    local_heads = key_absorb.shape[0]
    nope_dim = key_absorb.shape[1]
    latent_dim = key_absorb.shape[2]
    rope_dim = query_rope.shape[1] // local_heads
    group_rows = query_nope.shape[0]
    requests = latent_cache.shape[0]
    context = latent_cache.shape[1]
    nope_query = query_nope.reshape(group_rows, local_heads, nope_dim)
    absorbed = jnp.einsum(
        "rhn,hnl->rhl", nope_query, key_absorb, preferred_element_type=jnp.float32
    ).astype(jnp.bfloat16)
    rope_query = query_rope.reshape(group_rows, local_heads, rope_dim)
    absorbed, rope_query = (
        lax.all_to_all(absorbed, "tensor", split_axis=0, concat_axis=1, tiled=True),
        lax.all_to_all(rope_query, "tensor", split_axis=0, concat_axis=1, tiled=True),
    )
    queries = jnp.concatenate([absorbed, rope_query], axis=2)
    score_scale = 1.0 / math.sqrt(nope_dim + rope_dim)
    scores = (
        jnp.einsum("rhc,rpc->rhp", queries, latent_cache, preferred_element_type=jnp.float32)
        * score_scale
    )
    own_score = (
        jnp.einsum("rhc,rc->rh", queries, new_latent, preferred_element_type=jnp.float32)
        * score_scale
    )
    in_range = lax.broadcasted_iota(jnp.int32, (requests, context), 1) < context_lengths[:, None]
    scores = jnp.where(in_range[:, None, :], scores, -jnp.inf)
    row_max = jnp.maximum(jnp.max(scores, axis=2), own_score)
    exp_scores = jnp.exp(scores - row_max[:, :, None])
    own_expo = jnp.exp(own_score - row_max)
    denom_sum = jnp.sum(exp_scores, axis=2) + own_expo
    weights = (exp_scores / denom_sum[:, :, None]).astype(jnp.bfloat16)
    own_weight = (own_expo / denom_sum).astype(jnp.bfloat16)
    attended = jnp.einsum(
        "rhp,rpl->rhl", weights, latent_cache[:, :, :latent_dim], preferred_element_type=jnp.float32
    )
    attended = attended + own_weight.astype(jnp.float32)[:, :, None] * new_latent[
        :, None, :latent_dim
    ].astype(jnp.float32)
    attended = attended.astype(jnp.bfloat16)
    attended = lax.all_to_all(attended, "tensor", split_axis=1, concat_axis=0, tiled=True)
    head_out = jnp.einsum(
        "rhl,hlv->rhv", attended, value_absorb, preferred_element_type=jnp.float32
    ).astype(jnp.bfloat16)
    head_out = head_out.reshape(group_rows, -1)
    partial_value = jnp.dot(
        lax.all_gather(head_out, "expert", axis=0, tiled=True),
        out_proj,
        preferred_element_type=jnp.float32,
    )
    local_width = out_proj.shape[1]
    partial_value = partial_value.reshape(expert_count, tensor_count, requests, local_width)
    summed = lax.psum(partial_value.astype(jnp.bfloat16), "tensor").astype(jnp.float32)
    summed = lax.dynamic_index_in_dim(summed, lax.axis_index("tensor"), 1, keepdims=False)
    attn_rows = lax.all_to_all(
        summed.astype(jnp.bfloat16), "expert", split_axis=0, concat_axis=2, tiled=True
    )[0]
    hidden = residual.astype(jnp.float32) + attn_rows.astype(jnp.float32)
    normed = hidden * lax.rsqrt(jnp.mean(hidden * hidden, axis=1, keepdims=True) + 1e-06)
    normed = (normed * norm_gain.astype(jnp.float32)[None, :]).astype(jnp.bfloat16)
    model_width = normed.shape[1]
    experts_all = expert_count * expert_gate.shape[0]
    picks_each = routes.shape[1]
    capacity = min(requests, 2 * -(-(requests * picks_each) // experts_all))
    flat_routes = routes.reshape(-1)
    pair_count = flat_routes.shape[0]
    earlier_mask = lax.broadcasted_iota(
        jnp.int32, (pair_count, pair_count), 1
    ) < lax.broadcasted_iota(jnp.int32, (pair_count, pair_count), 0)
    slot_index = jnp.sum(
        ((flat_routes[:, None] == flat_routes[None, :]) & earlier_mask).astype(jnp.int32), axis=1
    )
    target = (flat_routes * capacity + slot_index).reshape(requests, picks_each)
    places = lax.broadcasted_iota(jnp.int32, (experts_all * capacity, requests, picks_each), 0)
    dispatch_table = jnp.any(places == target[None, :, :], axis=2).astype(jnp.bfloat16)
    columns = lax.broadcasted_iota(jnp.int32, (requests, picks_each, experts_all * capacity), 2)
    combine_table = jnp.sum(
        jnp.where(columns == target[:, :, None], gate_weights[:, :, None], 0.0), axis=1
    )
    outgoing = jnp.dot(dispatch_table, normed, preferred_element_type=jnp.float32).astype(
        jnp.bfloat16
    )
    outgoing = outgoing.reshape(experts_all, capacity, model_width)
    arrived = lax.all_to_all(outgoing, "expert", split_axis=0, concat_axis=0, tiled=True)
    token_rows = lax.all_gather(arrived.reshape(-1, model_width), "tensor", axis=0, tiled=True)
    gate_part = jnp.dot(token_rows, expert_gate[0], preferred_element_type=jnp.float32)
    up_part = jnp.dot(token_rows, expert_up[0], preferred_element_type=jnp.float32)
    active = (jax.nn.silu(gate_part) * up_part).astype(jnp.bfloat16)
    summed_rows = lax.psum_scatter(
        jnp.dot(active, expert_down[0], preferred_element_type=jnp.float32).astype(jnp.bfloat16),
        "tensor",
        scatter_dimension=0,
        tiled=True,
    ).astype(jnp.float32)
    summed_rows = summed_rows.astype(jnp.bfloat16).reshape(expert_count, capacity, model_width)
    expert_out = lax.all_to_all(summed_rows, "expert", split_axis=0, concat_axis=0, tiled=True)
    routed_sum = jnp.dot(
        combine_table,
        expert_out.reshape(-1, model_width).astype(jnp.float32),
        precision=lax.Precision.HIGHEST,
    )
    return (hidden + routed_sum).astype(jnp.bfloat16)


def solution(mesh):
    placed = (
        P("expert", "tensor"),
        P("expert", "tensor"),
        P("tensor", None, None),
        P(("expert", "tensor"), None, None),
        P(("expert", "tensor"), None),
        P(("expert", "tensor")),
        P("tensor", None, None),
        P("tensor", "expert"),
        P(("expert", "tensor"), None),
        P(),
        P(("expert", "tensor"), None),
        P(("expert", "tensor"), None),
        P("expert", None, "tensor"),
        P("expert", None, "tensor"),
        P("expert", "tensor", None),
    )
    return jax.shard_map(
        per_device,
        mesh=mesh,
        in_specs=placed,
        out_specs=P(("expert", "tensor"), None),
        check_vma=False,
    )
```

profile of v0, /device:TPU:0, one launch (start us, length us, event | category | flops | bytes accessed | tf_op | source)
XLA Modules:
  0.0 436.6 jit_solution(9570119983695232010)
XLA Ops:
  8.7 4.5 %all-to-all-start.1 = ((bf16[4,2,8192]{2,1,0:T(2,128)(2,1)}), bf16[4,2,8192]{2,1,0:T(2,128)(2,1)S(1)}, u32[]{:S(2)}, u32[]{:S(2)}) async-start(bf16[4,2,8192]{2,1,0:T(2,128)(2,1)} %reshape.85), calls=%async_computation.1 | async-start | bytes 262144 | tf_op jit(solution)/shard_map/all_to_all | solution.py:42
  13.3 3.0 fusion.12
  19.3 3.5 all-to-all-start
  23.3 13.8 %all-to-all-done = bf16[32,32,512]{2,1,0:T(8,128)(2,1)S(1)} async-done(((bf16[32,32,512]{2,1,0:T(8,128)(2,1)}), bf16[32,32,512]{2,1,0:T(8,128)(2,1)S(1)}, u32[]{:S(2)}, u32[]{:S(2)}) %all-to-all-start) | async-done | bytes 1048608 | tf_op jit(solution)/shard_map/all_to_all | solution.py:41
  38.2 1.6 copy.58
  40.1 3.7 fusion.8
  44.5 1.9 add_convert_fusion
  47.0 16.0 %all_to_all.73 = bf16[8,128,512]{2,0,1:T(8,128)(2,1)S(1)} all-to-all(bf16[8,128,512]{2,0,1:T(8,128)(2,1)S(1)} %copy.61), channel_id=1, replica_groups=mesh['expert'=32,'tensor'=4] {'tensor'}, dimensions={1} | all-to-all | bytes 2097152 | tf_op jit(solution)/shard_map/all_to_all | solution.py:69
  64.6 53.5 %all-gather.3.cloned.1.call-done = bf16[1024,4096]{1,0:T(8,128)(2,1)} async-done(((bf16[32,4096]{1,0:T(8,128)(2,1)}), bf16[1024,4096]{1,0:T(8,128)(2,1)}) %all-gather.3.cloned.1.call-update) | async-done | bytes 8388624 | tf_op jit(solution)/shard_map/all_gather | solution.py:75
  118.0 6.0 %convolution_convert_fusion.3 = bf16[1024,224]{0,1:T(8,128)(2,1)S(1)} fusion(bf16[1024,4096]{1,0:T(8,128)(2,1)} %all-gather.3.cloned.1.call-done, bf16[4096,224]{0,1:T(8,128)(2,1)S(1)} %copy-done), kind=kOutput, calls=%fused_computation.19 | convolution fusion | flops 1879277568 | bytes 10682368 | tf_op jit(solution)/shard_map/dot_general | solution.py:74
  125.5 42.3 %all-reduce.2.cloned.1.call-done = bf16[32,4,8,224]{3,2,1,0:T(8,128)(2,1)} async-done(((bf16[32,4,8,224]{3,2,1,0:T(8,128)(2,1)}), bf16[32,4,8,224]{3,2,1,0:T(8,128)(2,1)}) %all-reduce.2.cloned.1.call-update) | async-done | bytes 458768 | tf_op jit(solution)/shard_map/psum | solution.py:81
  169.3 7.2 %all-to-all-start.3 = ((bf16[32,8,224]{2,1,0:T(8,128)(2,1)}), bf16[32,8,224]{2,1,0:T(8,128)(2,1)S(1)}, u32[]{:S(2)}, u32[]{:S(2)}) async-start(bf16[32,8,224]{2,1,0:T(8,128)(2,1)} %fusion.34), calls=%async_computation.3 | async-start | bytes 262144 | tf_op jit(solution)/shard_map/all_to_all | solution.py:83
  176.7 7.7 %all-to-all-done.3 = bf16[32,8,224]{2,1,0:T(8,128)(2,1)S(1)} async-done(((bf16[32,8,224]{2,1,0:T(8,128)(2,1)}), bf16[32,8,224]{2,1,0:T(8,128)(2,1)S(1)}, u32[]{:S(2)}, u32[]{:S(2)}) %all-to-all-start.3) | async-done | bytes 114720 | tf_op jit(solution)/shard_map/all_to_all | solution.py:83
  185.6 1.7 reshape.77
  187.2 29.0 %all_to_all.74 = bf16[32,4,7168]{2,1,0:T(4,128)(2,1)S(1)} all-to-all(bf16[32,4,7168]{2,1,0:T(4,128)(2,1)} %reshape.77), channel_id=1, replica_groups=mesh['expert'=32,'tensor'=4] {'expert'}, dimensions={0} | all-to-all | bytes 3670016 | tf_op jit(solution)/shard_map/all_to_all | solution.py:112
  218.0 71.9 %all-gather.5.cloned.1.call-done = bf16[512,7168]{1,0:T(8,128)(2,1)} async-done(((bf16[128,7168]{1,0:T(8,128)(2,1)}), bf16[512,7168]{1,0:T(8,128)(2,1)}) %all-gather.5.cloned.1.call-update) | async-done | bytes 7340048 | tf_op jit(solution)/shard_map/all_gather | solution.py:113
  290.0 6.2 %fusion.6 = f32[512,256]{1,0:T(8,128)S(1)} fusion(bf16[512,7168]{1,0:T(8,128)(2,1)} %all-gather.5.cloned.1.call-done, bf16[1,7168,256]{2,1,0:T(8,128)(2,1)} %param.27), kind=kOutput, calls=%fused_computation.9 | convolution fusion | flops 1879048192 | bytes 11534336 | tf_op jit(solution)/shard_map/dot_general | solution.py:114
  296.1 16.0 %convolution_convert_fusion = bf16[512,7168]{1,0:T(8,128)(2,1)} fusion(bf16[1,256,7168]{2,1,0:T(8,128)(2,1)} %param.29, bf16[512,7168]{1,0:T(8,128)(2,1)} %all-gather.5.cloned.1.call-done, bf16[1,7168,256]{2,1,0:T(8,128)(2,1)} %param.28, f32[512,256]{1,0:T(8,128)S(1)} %fusion.6), kind=kOutput, calls=%fused_computation | convolution fusion | flops 3762552832 | bytes 22544384 | tf_op jit(solution)/shard_map/dot_general | solution.py:118
  312.2 73.5 %reduce-scatter.2.cloned.1.call-done = bf16[128,7168]{1,0:T(8,128)(2,1)} async-done(((bf16[512,7168]{1,0:T(8,128)(2,1)}), bf16[128,7168]{1,0:T(8,128)(2,1)}) %reduce-scatter.2.cloned.1.call-update) | async-done | bytes 1835024 | tf_op jit(solution)/shard_map/reduce_scatter | solution.py:117
  385.6 4.1 reshape.79
  389.7 7.5 %all-to-all-start.5 = ((bf16[32,4,7168]{2,1,0:T(4,128)(2,1)}), bf16[32,4,7168]{2,1,0:T(4,128)(2,1)}, u32[]{:S(2)}, u32[]{:S(2)}) async-start(bf16[32,4,7168]{2,1,0:T(4,128)(2,1)} %reshape.79), calls=%async_computation.6 | async-start | bytes 3670016 | tf_op jit(solution)/shard_map/all_to_all | solution.py:124
  397.3 25.9 %all-to-all-done.5 = bf16[32,4,7168]{2,1,0:T(4,128)(2,1)} async-done(((bf16[32,4,7168]{2,1,0:T(4,128)(2,1)}), bf16[32,4,7168]{2,1,0:T(4,128)(2,1)}, u32[]{:S(2)}, u32[]{:S(2)}) %all-to-all-start.5) | async-done | bytes 1835040 | tf_op jit(solution)/shard_map/all_to_all | solution.py:124
  423.2 3.9 reshape.80
  427.1 3.0 fusion
  (64 shorter events, 15.9 us)
Async XLA Ops:
  6.5 111.5 %copy-start = (bf16[4096,224]{0,1:T(8,128)(2,1)S(1)}, bf16[4096,224]{0,1:T(8,128)(2,1)}, u32[]{:S(2)}) copy-start(bf16[4096,224]{0,1:T(8,128)(2,1)} %param.22) | copy-start | bytes 5505028
  8.7 10.5 %all-to-all-start.1 = ((bf16[4,2,8192]{2,1,0:T(2,128)(2,1)}), bf16[4,2,8192]{2,1,0:T(2,128)(2,1)S(1)}, u32[]{:S(2)}, u32[]{:S(2)}) async-start(bf16[4,2,8192]{2,1,0:T(2,128)(2,1)} %reshape.85), calls=%async_computation.1 | async-start | bytes 262144 | tf_op jit(solution)/shard_map/all_to_all | solution.py:42
  16.2 6.6 %copy-start.8 = (s32[8]{0:T(128)S(1)}, s32[8]{0:T(128)}, u32[]{:S(2)}) copy-start(s32[8]{0:T(128)} %param.20) | copy-start | bytes 100
  16.3 6.7 %copy-start.6 = (bf16[8,576]{1,0:T(8,128)(2,1)S(1)}, bf16[8,576]{1,0:T(8,128)(2,1)}, u32[]{:S(2)}) copy-start(bf16[8,576]{1,0:T(8,128)(2,1)} %param.19) | copy-start | bytes 27652
  19.3 17.9 %all-to-all-start = ((bf16[32,32,512]{2,1,0:T(8,128)(2,1)}), bf16[32,32,512]{2,1,0:T(8,128)(2,1)S(1)}, u32[]{:S(2)}, u32[]{:S(2)}) async-start(bf16[32,32,512]{2,1,0:T(8,128)(2,1)} %copy.55), calls=%async_computation | async-start | bytes 2097152 | tf_op jit(solution)/shard_map/all_to_all | solution.py:41
  22.8 95.3 %all-gather.3.cloned.1.call-start = ((), (), s32[]{:S(2)}) async-start(), calls=%async_computation.7 | async-start | bytes 8650752 | tf_op jit(solution)/shard_map/all_gather | solution.py:75
  39.8 4.6 %slice-start = ((s8[4718592]{0:T(1024)(128)(4,1)}), s8[4194304]{0:T(1024)(128)(4,1)S(1)}, s32[]{:S(2)}) async-start(s8[4718592]{0:T(1024)(128)(4,1)} %bitcast.77), calls=%async_computation.11 | async-start | bytes 8388608
  40.1 4.4 slice-start.1
  46.4 16.6 %copy-start.2 = (bf16[32,512,128]{2,1,0:T(8,128)(2,1)S(1)}, bf16[32,512,128]{2,1,0:T(8,128)(2,1)}, u32[]{:S(2)}) copy-start(bf16[32,512,128]{2,1,0:T(8,128)(2,1)} %param.21) | copy-start | bytes 12582916
  64.5 60.6 %copy-start.4 = (s32[8,8]{1,0:T(8,128)S(1)}, s32[8,8]{1,0:T(8,128)}, u32[]{:S(2)}) copy-start(s32[8,8]{1,0:T(8,128)} %param.25) | copy-start | bytes 772
  64.5 60.9 %copy-start.5 = (bf16[7168]{0:T(1024)(128)(2,1)S(1)}, bf16[7168]{0:T(1024)(128)(2,1)}, u32[]{:S(2)}) copy-start(bf16[7168]{0:T(1024)(128)(2,1)} %param.24) | copy-start | bytes 43012
  64.5 103.2 %all-reduce.2.cloned.1.call-start = ((), (), s32[]{:S(2)}) async-start(), calls=%async_computation.8 | async-start | bytes 1048576 | tf_op jit(solution)/shard_map/psum | solution.py:81
  124.0 60.6 %copy-start.3 = (bf16[8,7168]{1,0:T(8,128)(2,1)S(1)}, bf16[8,7168]{1,0:T(8,128)(2,1)}, u32[]{:S(2)}) copy-start(bf16[8,7168]{1,0:T(8,128)(2,1)} %param.23) | copy-start | bytes 344068
  169.3 15.1 %all-to-all-start.3 = ((bf16[32,8,224]{2,1,0:T(8,128)(2,1)}), bf16[32,8,224]{2,1,0:T(8,128)(2,1)S(1)}, u32[]{:S(2)}, u32[]{:S(2)}) async-start(bf16[32,8,224]{2,1,0:T(8,128)(2,1)} %fusion.34), calls=%async_computation.3 | async-start | bytes 262144 | tf_op jit(solution)/shard_map/all_to_all | solution.py:83
  176.5 113.4 %all-gather.5.cloned.1.call-start = ((), (), s32[]{:S(2)}) async-start(), calls=%async_computation.9 | async-start | bytes 9175040 | tf_op jit(solution)/shard_map/all_gather | solution.py:113
  217.8 167.8 %reduce-scatter.2.cloned.1.call-start = ((), (), s32[]{:S(2)}) async-start(), calls=%async_computation.10 | async-start | bytes 9175040 | tf_op jit(solution)/shard_map/reduce_scatter | solution.py:117
  389.7 7.5 %copy-start.7 = (f32[8,8]{1,0:T(8,128)S(1)}, f32[8,8]{1,0:T(8,128)}, u32[]{:S(2)}) copy-start(f32[8,8]{1,0:T(8,128)} %param.26) | copy-start | bytes 772
  389.7 33.5 %all-to-all-start.5 = ((bf16[32,4,7168]{2,1,0:T(4,128)(2,1)}), bf16[32,4,7168]{2,1,0:T(4,128)(2,1)}, u32[]{:S(2)}, u32[]{:S(2)}) async-start(bf16[32,4,7168]{2,1,0:T(4,128)(2,1)} %reshape.79), calls=%async_computation.6 | async-start | bytes 3670016 | tf_op jit(solution)/shard_map/all_to_all | solution.py:124
  397.2 32.9 %copy-start.1 = (bf16[4096,224]{0,1:T(8,128)(2,1)S(1)}, bf16[4096,224]{0,1:T(8,128)(2,1)}, u32[]{:S(2)}) copy-start(bf16[4096,224]{0,1:T(8,128)(2,1)} %param.22) | copy-start | bytes 5505028
Sparse Core Ops, SparseCore 0:
  64.6 53.3 all-gather.2
  125.2 42.4 all-reduce.1
  217.9 71.9 all-gather.4
  312.3 73.2 reduce-scatter.1
where the time goes:
time: 438 us; the launch traced here: 437 us
  waiting for transfers between devices  290 us (66%)
  blocking collectives  45.1 us (10%)
  matrix products  41.3 us (9%)
  starting transfers between devices  23.1 us (5%)
  local copies, waits for them, and re-layouts  20.8 us (5%)
  between operations  13.4 us (3%)
    reduce_scatter x1, waiting for transfers between devices, per_device(): lax.psum_scatter(jnp.dot(active, expert_down[0], preferred_element_type=j...  73.5 us
    all_gather x1, waiting for transfers between devices, per_device(): lax.all_gather(arrived.reshape(-1, model_width), 'tensor', axis=0, tiled=...  71.9 us
    all_gather x1, waiting for transfers between devices, per_device(): lax.all_gather(head_out, 'expert', axis=0, tiled=True)  53.5 us
    psum x1, waiting for transfers between devices, per_device(): lax.psum(partial_value.astype(jnp.bfloat16), 'tensor').astype(jnp.float32)  42.3 us
    all_to_all x1, blocking collectives, per_device(): lax.all_to_all(outgoing, 'expert', split_axis=0, concat_axis=0, tiled=True)  29 us
    all_to_all x1, waiting for transfers between devices, per_device(): lax.all_to_all(summed_rows, 'expert', split_axis=0, concat_axis=0, tiled=...  25.9 us
    all_to_all x1, blocking collectives, per_device(): lax.all_to_all(attended, 'tensor', split_axis=1, concat_axis=0, tiled=True)  16 us
    dot_general x1, matrix products, per_device(): jnp.dot(active, expert_down[0], preferred_element_type=jnp.float32)  16 us
  transfers between devices with their start and end apart: 8, of which 8 were waited for; matrix products, arithmetic and copies ran while one was open for 1% of the time, Pallas kernels for 0%

commit v1 on v0

--- a/solution.py
+++ b/solution.py
@@ -77,57 +77,34 @@
         preferred_element_type=jnp.float32,
     )
     local_width = out_proj.shape[1]
-    partial_value = partial_value.reshape(expert_count, tensor_count, requests, local_width)
-    summed = lax.psum(partial_value.astype(jnp.bfloat16), "tensor").astype(jnp.float32)
-    summed = lax.dynamic_index_in_dim(summed, lax.axis_index("tensor"), 1, keepdims=False)
+    partial_value = partial_value.astype(jnp.bfloat16).reshape(
+        expert_count, tensor_count, requests, local_width
+    )
+    partial_value = jnp.swapaxes(partial_value, 0, 1).reshape(-1, local_width)
+    summed = lax.psum_scatter(partial_value, "tensor", scatter_dimension=0, tiled=True)
+    summed = summed.reshape(expert_count, requests, local_width)
     attn_rows = lax.all_to_all(
-        summed.astype(jnp.bfloat16), "expert", split_axis=0, concat_axis=2, tiled=True
+        summed, "expert", split_axis=0, concat_axis=2, tiled=True
     )[0]
     hidden = residual.astype(jnp.float32) + attn_rows.astype(jnp.float32)
     normed = hidden * lax.rsqrt(jnp.mean(hidden * hidden, axis=1, keepdims=True) + 1e-06)
     normed = (normed * norm_gain.astype(jnp.float32)[None, :]).astype(jnp.bfloat16)
-    model_width = normed.shape[1]
-    experts_all = expert_count * expert_gate.shape[0]
-    picks_each = routes.shape[1]
-    capacity = min(requests, 2 * -(-(requests * picks_each) // experts_all))
-    flat_routes = routes.reshape(-1)
-    pair_count = flat_routes.shape[0]
-    earlier_mask = lax.broadcasted_iota(
-        jnp.int32, (pair_count, pair_count), 1
-    ) < lax.broadcasted_iota(jnp.int32, (pair_count, pair_count), 0)
-    slot_index = jnp.sum(
-        ((flat_routes[:, None] == flat_routes[None, :]) & earlier_mask).astype(jnp.int32), axis=1
+    tokens = lax.all_gather(normed, ("expert", "tensor"), axis=0, tiled=True)
+    experts = lax.broadcasted_iota(jnp.int32, (1, 1, expert_count), 2)
+    table = jnp.sum(
+        jnp.where(routes[:, :, None] == experts, gate_weights[:, :, None], 0.0), axis=1
     )
-    target = (flat_routes * capacity + slot_index).reshape(requests, picks_each)
-    places = lax.broadcasted_iota(jnp.int32, (experts_all * capacity, requests, picks_each), 0)
-    dispatch_table = jnp.any(places == target[None, :, :], axis=2).astype(jnp.bfloat16)
-    columns = lax.broadcasted_iota(jnp.int32, (requests, picks_each, experts_all * capacity), 2)
-    combine_table = jnp.sum(
-        jnp.where(columns == target[:, :, None], gate_weights[:, :, None], 0.0), axis=1
+    table = lax.all_gather(table, ("expert", "tensor"), axis=0, tiled=True)
+    mine = lax.broadcasted_iota(jnp.int32, (1, expert_count), 1) == lax.axis_index("expert")
+    weight = jnp.sum(jnp.where(mine, table, 0.0), axis=1, keepdims=True)
+    gate_part = jnp.dot(tokens, expert_gate[0], preferred_element_type=jnp.float32)
+    up_part = jnp.dot(tokens, expert_up[0], preferred_element_type=jnp.float32)
+    active = (jax.nn.silu(gate_part) * up_part * weight).astype(jnp.bfloat16)
+    partial_out = jnp.dot(active, expert_down[0], preferred_element_type=jnp.float32)
+    routed_sum = lax.psum_scatter(
+        partial_out.astype(jnp.bfloat16), ("expert", "tensor"), scatter_dimension=0, tiled=True
     )
-    outgoing = jnp.dot(dispatch_table, normed, preferred_element_type=jnp.float32).astype(
-        jnp.bfloat16
-    )
-    outgoing = outgoing.reshape(experts_all, capacity, model_width)
-    arrived = lax.all_to_all(outgoing, "expert", split_axis=0, concat_axis=0, tiled=True)
-    token_rows = lax.all_gather(arrived.reshape(-1, model_width), "tensor", axis=0, tiled=True)
-    gate_part = jnp.dot(token_rows, expert_gate[0], preferred_element_type=jnp.float32)
-    up_part = jnp.dot(token_rows, expert_up[0], preferred_element_type=jnp.float32)
-    active = (jax.nn.silu(gate_part) * up_part).astype(jnp.bfloat16)
-    summed_rows = lax.psum_scatter(
-        jnp.dot(active, expert_down[0], preferred_element_type=jnp.float32).astype(jnp.bfloat16),
-        "tensor",
-        scatter_dimension=0,
-        tiled=True,
-    ).astype(jnp.float32)
-    summed_rows = summed_rows.astype(jnp.bfloat16).reshape(expert_count, capacity, model_width)
-    expert_out = lax.all_to_all(summed_rows, "expert", split_axis=0, concat_axis=0, tiled=True)
-    routed_sum = jnp.dot(
-        combine_table,
-        expert_out.reshape(-1, model_width).astype(jnp.float32),
-        precision=lax.Precision.HIGHEST,
-    )
-    return (hidden + routed_sum).astype(jnp.bfloat16)
+    return (hidden + routed_sum.astype(jnp.float32)).astype(jnp.bfloat16)
 
 
 def solution(mesh):

time: 438 us -> 930 us (2.12)
  waiting for transfers between devices: 290 us -> 777 us
  blocking collectives: 45.1 us -> 72.7 us
    reduce_scatter x1 -> x2, waiting for transfers between devices: 73.5 us -> 683 us  [the longest x1 662 us: per_device(): lax.psum_scatter(partial_out.astype(jnp.bfloat16), ('expert', 'tensor'),...]
    all_gather x0 -> x1, blocking collectives: none -> 56.7 us  [per_device(): table = lax.all_gather(table, ('expert', 'tensor'), axis=0, tiled=True)]
    all_gather x1, waiting for transfers between devices: 71.9 us -> 17 us  [per_device(): tokens = lax.all_gather(normed, ('expert', 'tensor'), axis=0, tiled=True)]
    psum x1 -> x0, waiting for transfers between devices: 42.3 us -> none  [per_device(): lax.psum(partial_value.astype(jnp.bfloat16), 'tensor').astype(jnp.float32)]
    all_to_all x1 -> x0, blocking collectives: 29 us -> none  [per_device(): lax.all_to_all(outgoing, 'expert', split_axis=0, concat_axis=0, tiled=True)]
    all_to_all x2 -> x1, waiting for transfers between devices: 33.6 us -> 7.79 us  [per_device(): lax.all_to_all(summed, 'expert', split_axis=0, concat_axis=2, tiled=True)[0]]
    reshape x4 -> x0, local copies, waits for them, and re-layouts: 11.2 us -> none  [the longest x1 4.08 us: per_device(): summed_rows.astype(jnp.bfloat16)]
  transfers between devices with their start and end apart: 8 -> 7, of which waited for: 8 -> 7; matrix products, arithmetic and copies ran while one was open for 1% -> 1% of each run, Pallas kernels for 0% -> 0%
where the time goes in v1:
time: 930 us
  waiting for transfers between devices  777 us (84%)
  blocking collectives  72.7 us (8%)
  matrix products  35.7 us (4%)
  starting transfers between devices  15.5 us (2%)
  between operations  13.4 us (1%)
  local copies, waits for them, and re-layouts  12 us (1%)
    reduce_scatter x1, waiting for transfers between devices, per_device(): lax.psum_scatter(partial_out.astype(jnp.bfloat16), ('expert', 'tensor'),...  662 us
    all_gather x1, blocking collectives, per_device(): table = lax.all_gather(table, ('expert', 'tensor'), axis=0, tiled=True)  56.7 us
    all_gather x1, waiting for transfers between devices, per_device(): lax.all_gather(head_out, 'expert', axis=0, tiled=True)  53.5 us
    reduce_scatter x1, waiting for transfers between devices, per_device(): lax.psum_scatter(partial_value, 'tensor', scatter_dimension=0, tiled=True)  21.1 us
  transfers between devices with their start and end apart: 7, of which 7 were waited for; matrix products, arithmetic and copies ran while one was open for 1% of the time, Pallas kernels for 0%

profile of v1, /device:TPU:0, one launch (start us, length us, event | category | flops | bytes accessed | tf_op | source)
XLA Modules:
  0.0 929.7 jit_solution(15227757218214059741)
XLA Ops:
  6.5 1.3 reshape.61
  8.7 4.5 all-to-all-start.1
  13.3 2.9 fusion.17
  16.3 1.6 copy.57
  17.8 1.4 all-to-all-done.1
  19.3 3.5 all-to-all-start
  23.3 13.8 %all-to-all-done = bf16[32,32,512]{2,1,0:T(8,128)(2,1)S(1)} async-done(((bf16[32,32,512]{2,1,0:T(8,128)(2,1)}), bf16[32,32,512]{2,1,0:T(8,128)(2,1)S(1)}, u32[]{:S(2)}, u32[]{:S(2)}) %all-to-all-start) | async-done | bytes 1048608 | tf_op jit(solution)/shard_map/all_to_all | solution.py:41
  38.2 1.6 copy.60
  40.1 3.7 fusion.7
  44.5 1.9 add_convert_fusion
  47.0 16.0 %all_to_all.63 = bf16[8,128,512]{2,0,1:T(8,128)(2,1)S(1)} all-to-all(bf16[8,128,512]{2,0,1:T(8,128)(2,1)S(1)} %copy.63), channel_id=1, replica_groups=mesh['expert'=32,'tensor'=4] {'tensor'}, dimensions={1} | all-to-all | bytes 2097152 | tf_op jit(solution)/shard_map/all_to_all | solution.py:69
  64.6 53.5 %all-gather.3.cloned.1.call-done = bf16[1024,4096]{1,0:T(8,128)(2,1)} async-done(((bf16[32,4096]{1,0:T(8,128)(2,1)}), bf16[1024,4096]{1,0:T(8,128)(2,1)}) %all-gather.3.cloned.1.call-update) | async-done | bytes 8388624 | tf_op jit(solution)/shard_map/all_gather | solution.py:75
  118.1 6.0 convolution_convert_fusion.2
  125.2 21.1 %reduce-scatter.3.cloned.1.call-done = bf16[256,224]{1,0:T(8,128)(2,1)} async-done(((bf16[1024,224]{1,0:T(8,128)(2,1)}), bf16[256,224]{1,0:T(8,128)(2,1)}) %reduce-scatter.3.cloned.1.call-update) | async-done | bytes 114704 | tf_op jit(solution)/shard_map/reduce_scatter | solution.py:84
  146.2 7.2 all-to-all-start.3
  153.6 7.8 all-to-all-done.3
  162.8 56.7 %all_gather.11 = f32[1024,32]{1,0:T(8,128)S(1)} all-gather(f32[8,32]{1,0:T(8,128)S(1)} %select_reduce_fusion.1), channel_id=1, replica_groups=mesh['expert'=32,'tensor'=4] {'expert','tensor'}, dimensions={0}, use_global_device_ids=true | all-gather | bytes 132096 | tf_op jit(solution)/shard_map/all_gather | solution.py:97
  219.7 17.0 %all-gather.5.cloned.1.call-done = bf16[1024,7168]{1,0:T(8,128)(2,1)} async-done(((bf16[8,7168]{1,0:T(8,128)(2,1)}), bf16[1024,7168]{1,0:T(8,128)(2,1)}) %all-gather.5.cloned.1.call-update) | async-done | bytes 14680080 | tf_op jit(solution)/shard_map/all_gather | solution.py:92
  236.7 8.9 fusion.5
  245.6 1.5 copy-done.10
  248.1 4.0 fusion.18
  252.2 7.3 convolution_convert_fusion
  259.5 662.1 %reduce-scatter.5.cloned.1.call-done = bf16[8,7168]{1,0:T(8,128)(2,1)} async-done(((bf16[1024,7168]{1,0:T(8,128)(2,1)}), bf16[8,7168]{1,0:T(8,128)(2,1)}) %reduce-scatter.5.cloned.1.call-update) | async-done | bytes 114704 | tf_op jit(solution)/shard_map/reduce_scatter | solution.py:104
  921.6 1.6 add_convert_fusion.1
  (62 shorter events, 9.3 us)
Async XLA Ops:
  6.5 111.5 %copy-start = (bf16[4096,224]{0,1:T(8,128)(2,1)S(1)}, bf16[4096,224]{0,1:T(8,128)(2,1)}, u32[]{:S(2)}) copy-start(bf16[4096,224]{0,1:T(8,128)(2,1)} %param.22) | copy-start | bytes 5505028
  8.7 10.5 %all-to-all-start.1 = ((bf16[4,2,8192]{2,1,0:T(2,128)(2,1)}), bf16[4,2,8192]{2,1,0:T(2,128)(2,1)S(1)}, u32[]{:S(2)}, u32[]{:S(2)}) async-start(bf16[4,2,8192]{2,1,0:T(2,128)(2,1)} %reshape.70), calls=%async_computation.1 | async-start | bytes 262144 | tf_op jit(solution)/shard_map/all_to_all | solution.py:42
  16.2 6.6 copy-start.9
  16.3 6.7 copy-start.6
  19.3 17.9 %all-to-all-start = ((bf16[32,32,512]{2,1,0:T(8,128)(2,1)}), bf16[32,32,512]{2,1,0:T(8,128)(2,1)S(1)}, u32[]{:S(2)}, u32[]{:S(2)}) async-start(bf16[32,32,512]{2,1,0:T(8,128)(2,1)} %copy.57), calls=%async_computation | async-start | bytes 2097152 | tf_op jit(solution)/shard_map/all_to_all | solution.py:41
  22.8 95.3 %all-gather.3.cloned.1.call-start = ((), (), s32[]{:S(2)}) async-start(), calls=%async_computation.6 | async-start | bytes 8650752 | tf_op jit(solution)/shard_map/all_gather | solution.py:75
  39.8 4.6 slice-start
  40.1 4.4 slice-start.1
  46.4 16.6 %copy-start.2 = (bf16[32,512,128]{2,1,0:T(8,128)(2,1)S(1)}, bf16[32,512,128]{2,1,0:T(8,128)(2,1)}, u32[]{:S(2)}) copy-start(bf16[32,512,128]{2,1,0:T(8,128)(2,1)} %param.21) | copy-start | bytes 12582916
  64.5 81.7 %reduce-scatter.3.cloned.1.call-start = ((), (), s32[]{:S(2)}) async-start(), calls=%async_computation.7 | async-start | bytes 655360 | tf_op jit(solution)/shard_map/reduce_scatter | solution.py:84
  124.1 29.5 %copy-start.5 = (bf16[7168]{0:T(1024)(128)(2,1)S(1)}, bf16[7168]{0:T(1024)(128)(2,1)}, u32[]{:S(2)}) copy-start(bf16[7168]{0:T(1024)(128)(2,1)} %param.24) | copy-start | bytes 43012
  124.1 37.6 %copy-start.4 = (bf16[8,7168]{1,0:T(8,128)(2,1)S(1)}, bf16[8,7168]{1,0:T(8,128)(2,1)}, u32[]{:S(2)}) copy-start(bf16[8,7168]{1,0:T(8,128)(2,1)} %param.23) | copy-start | bytes 344068
  124.3 38.4 %copy-start.7 = (f32[8,8]{1,0:T(8,128)S(1)}, f32[8,8]{1,0:T(8,128)}, u32[]{:S(2)}) copy-start(f32[8,8]{1,0:T(8,128)} %param.26) | copy-start | bytes 772
  124.3 38.4 %copy-start.8 = (s32[8,8]{1,0:T(8,128)S(1)}, s32[8,8]{1,0:T(8,128)}, u32[]{:S(2)}) copy-start(s32[8,8]{1,0:T(8,128)} %param.25) | copy-start | bytes 772
  146.2 15.1 %all-to-all-start.3 = ((bf16[32,8,224]{2,1,0:T(8,128)(2,1)}), bf16[32,8,224]{2,1,0:T(8,128)(2,1)S(1)}, u32[]{:S(2)}, u32[]{:S(2)}) async-start(bf16[32,8,224]{2,1,0:T(8,128)(2,1)} %bitcast.75), calls=%async_computation.4 | async-start | bytes 262144 | tf_op jit(solution)/shard_map/all_to_all | solution.py:86
  153.5 83.2 %all-gather.5.cloned.1.call-start = ((), (), s32[]{:S(2)}) async-start(), calls=%async_computation.8 | async-start | bytes 14794752 | tf_op jit(solution)/shard_map/all_gather | solution.py:92
  162.6 759.0 %reduce-scatter.5.cloned.1.call-start = ((), (), s32[]{:S(2)}) async-start(), calls=%async_computation.9 | async-start | bytes 14794752 | tf_op jit(solution)/shard_map/reduce_scatter | solution.py:104
  236.7 10.4 %copy-start.10 = (bf16[1024,7168]{1,0:T(8,128)(2,1)S(1)}, bf16[1024,7168]{1,0:T(8,128)(2,1)}, u32[]{:S(2)}) copy-start(bf16[1024,7168]{1,0:T(8,128)(2,1)} %all-gather.5.cloned.1.call-done) | copy-start | bytes 44040196
  236.7 11.4 %copy-start.11 = (bf16[1,7168,256]{2,1,0:T(8,128)(2,1)S(1)}, bf16[1,7168,256]{2,1,0:T(8,128)(2,1)}, u32[]{:S(2)}) copy-start(bf16[1,7168,256]{2,1,0:T(8,128)(2,1)} %param.28) | copy-start | bytes 11010052
  248.1 4.0 copy-start.3
  259.5 663.7 %copy-start.1 = (bf16[4096,224]{0,1:T(8,128)(2,1)S(1)}, bf16[4096,224]{0,1:T(8,128)(2,1)}, u32[]{:S(2)}) copy-start(bf16[4096,224]{0,1:T(8,128)(2,1)} %param.22) | copy-start | bytes 5505028
Sparse Core Ops, SparseCore 0:
  64.6 53.3 all-gather.2
  125.3 20.9 reduce-scatter.2
  162.7 73.9 all-gather.4
  259.6 661.9 reduce-scatter.4

commit v2 on v1

--- a/solution.py
+++ b/solution.py
@@ -1,9 +1,277 @@
-import math
-
-import jax
-import jax.numpy as jnp
+import functools, math
+import jax, jax.numpy as jnp
 from jax import lax
+from jax.experimental import pallas as pl
+from jax.experimental.pallas import tpu as pltpu
 from jax.sharding import PartitionSpec as P
+
+MESH = pl.DeviceIdType.MESH
+BF = jnp.bfloat16
+F32 = jnp.float32
+SIBLING = 6
+
+
+def place():
+    e, y = lax.axis_index("expert"), lax.axis_index("tensor")
+    return e // 8, y, (e // 2) % 4, e % 2
+
+
+def cube_bits(x, y, z):
+    out = []
+    for v in (y, x, z):
+        g = jnp.where(v >= 2, 5 - v, v)
+        out += [g // 2, g % 2]
+    return out
+
+
+def partner(x, y, z, c, d):
+    if d == SIBLING:
+        return ((x * 4 + z) * 2 + 1 - c, y)
+    at = [y, x, z]
+    v = at[d // 2]
+    at[d // 2] = 3 - v if d % 2 == 0 else v + 1 - 2 * (v % 2)
+    y, x, z = at
+    return ((x * 4 + z) * 2 + c, y)
+
+
+def meet(dims, x, y, z, c):
+    barrier = pltpu.get_barrier_semaphore()
+    for d in dims:
+        pl.semaphore_signal(barrier, inc=1, device_id=partner(x, y, z, c, d), device_id_type=MESH)
+    pl.semaphore_wait(barrier, len(dims))
+
+
+OUT_W = (640, 640, 640, 640, 512, 512)
+OUT_AT = (0, 640, 1280, 1920, 2560, 3072)
+
+
+def moe_out_kernel(act, down, out, ps, rb, r0, r1, r2, r3, r4, r5, sib_s, sib_r, st_s, st_r, fin):
+    x, y, z, c = place()
+    bits = cube_bits(x, y, z)
+    rs = (r0, r1, r2, r3, r4, r5)
+    meet(range(7), x, y, z, c)
+    sib = partner(x, y, z, c, SIBLING)
+
+    def cut(ref, p, fixed, lead=()):
+        idx = tuple(fixed[d] if d in fixed else slice(None) for d in range(6))
+        return ref.at[lead + idx + (slice(None), pl.ds(OUT_AT[p], OUT_W[p]))]
+
+    def product(p, which):
+        b = 1 - bits[p] if which == 0 else bits[p]
+
+        def one(side, carry):
+            half = jnp.where(side == 0, 1 - c, c)
+            rows = act[tuple(b if d == p else slice(None) for d in range(6))]
+            rows = rows.reshape(512, 256)
+            cols = pl.ds(pl.multiple_of(half * 3584 + OUT_AT[p], 128), OUT_W[p])
+            got = jnp.dot(rows, down[:, cols], preferred_element_type=F32).astype(BF)
+            cut(ps, p, {p: b}, (side,))[...] = got.reshape(2, 2, 2, 2, 2, 16, OUT_W[p])
+            return carry
+
+        lax.fori_loop(0, 2, one, 0)
+        copy = pltpu.make_async_remote_copy(
+            src_ref=cut(ps, p, {p: b}, (0,)), dst_ref=cut(rb, p, {p: b}),
+            send_sem=sib_s.at[which, p], recv_sem=sib_r.at[which, p],
+            device_id=sib, device_id_type=MESH)
+        copy.start()
+        return copy
+
+    def add(p, fixed, other):
+        here = cut(ps, p, fixed, (1,))
+        here[...] = (here[...].astype(F32) + other.astype(F32)).astype(BF)
+
+    sibs = {}
+    sends = {}
+
+    def send(p, s):
+        d = (p + s) % 6
+        fixed = {(p + k) % 6: bits[(p + k) % 6] for k in range(s)}
+        fixed[d] = 1 - bits[d]
+        free = 5 - s
+        copy = pltpu.make_async_remote_copy(
+            src_ref=cut(ps, p, fixed, (1,)),
+            dst_ref=rs[s].at[(slice(None),) * free + (slice(None), pl.ds(OUT_AT[p], OUT_W[p]))],
+            send_sem=st_s.at[s, p], recv_sem=st_r.at[s, p],
+            device_id=partner(x, y, z, c, d), device_id_type=MESH)
+        copy.start()
+        sends[p, s] = copy
+
+    for p in range(6):
+        sibs[0, p] = product(p, 0)
+        if p:
+            q = p - 1
+            sibs[0, q].wait_recv()
+            f = {q: 1 - bits[q]}
+            add(q, f, cut(rb, q, f)[...])
+            send(q, 0)
+    q = 5
+    sibs[0, q].wait_recv()
+    f = {q: 1 - bits[q]}
+    add(q, f, cut(rb, q, f)[...])
+    send(q, 0)
+    for p in range(6):
+        sibs[1, p] = product(p, 1)
+    for p in range(6):
+        sibs[1, p].wait_recv()
+        f = {p: bits[p]}
+        add(p, f, cut(rb, p, f)[...])
+    for s in range(6):
+        for p in range(6):
+            sends[p, s].wait_recv()
+            fixed = {(p + k) % 6: bits[(p + k) % 6] for k in range(s + 1)}
+            add(p, fixed, rs[s][(slice(None),) * (5 - s) + (slice(None), pl.ds(OUT_AT[p], OUT_W[p]))])
+            if s < 5:
+                send(p, s + 1)
+    me = ps.at[(1,) + tuple(bits)]
+    last = pltpu.make_async_remote_copy(
+        src_ref=me, dst_ref=fin.at[0], send_sem=sib_s.at[0, 6], recv_sem=sib_r.at[0, 6],
+        device_id=sib, device_id_type=MESH)
+    last.start()
+    out[c] = me[...]
+    last.wait_recv()
+    out[1 - c] = fin[0]
+    last.wait_send()
+    for p in range(6):
+        sibs[0, p].wait_send()
+        sibs[1, p].wait_send()
+        for s in range(6):
+            sends[p, s].wait_send()
+
+
+def moe_out(act, down, cid):
+    cube = (2,) * 6
+    return pl.pallas_call(
+        moe_out_kernel,
+        out_shape=jax.ShapeDtypeStruct((2, 16, 3584), BF),
+        in_specs=[pl.BlockSpec(memory_space=pltpu.VMEM)] * 2,
+        out_specs=pl.BlockSpec(memory_space=pltpu.VMEM),
+        scratch_shapes=[
+            pltpu.VMEM((2,) + cube + (16, 3584), BF),
+            pltpu.VMEM(cube + (16, 3584), BF),
+        ] + [pltpu.VMEM((2,) * (5 - s) + (16, 3584), BF) for s in range(6)] + [
+            pltpu.SemaphoreType.DMA((2, 7)), pltpu.SemaphoreType.DMA((2, 7)),
+            pltpu.SemaphoreType.DMA((6, 6)), pltpu.SemaphoreType.DMA((6, 6)),
+            pltpu.VMEM((1, 16, 3584), BF),
+        ],
+        compiler_params=pltpu.CompilerParams(collective_id=cid, has_side_effects=True, vmem_limit_bytes=56 << 20),
+        cost_estimate=pl.CostEstimate(flops=2 * 1024 * 256 * 7168, bytes_accessed=1 << 23, transcendentals=0),
+    )(act.reshape(cube + (16, 256)), down)
+
+
+ROW_AT = (0, 80, 160, 0, 80, 160)
+ROW_N = (80, 80, 64, 80, 80, 64)
+
+
+def moe_in_kernel(hid, sq, gate, up, act, own, buf, sqb, rows, accg, accu, st_s, st_r, sb_s, sb_r):
+    x, y, z, c = place()
+    bits = cube_bits(x, y, z)
+    yh, yl, xh, xl, zh, zl = bits
+    meet(range(7), x, y, z, c)
+    sib = partner(x, y, z, c, SIBLING)
+
+    def cut(p, known):
+        g = lambda d: slice(None) if d in known else bits[d]
+        if p == 6:
+            return sqb.at[g(0), g(1), g(2), g(3), g(4), g(5), c]
+        return buf.at[g(2), g(3), g(0), g(1), p // 3, g(4), g(5), c, pl.ds(ROW_AT[p], ROW_N[p]), :]
+
+    def fresh(p, s):
+        first = 2 if p == 6 else p
+        known = [(first + k) % 6 for k in range(max(s - 1, 0))]
+        if s == 0:
+            return cut(p, [])
+        d = (first + s - 1) % 6
+        g = lambda e: slice(None) if e in known else (1 - bits[e] if e == d else bits[e])
+        if p == 6:
+            return sqb.at[g(0), g(1), g(2), g(3), g(4), g(5), c]
+        return buf.at[g(2), g(3), g(0), g(1), p // 3, g(4), g(5), c, pl.ds(ROW_AT[p], ROW_N[p]), :]
+
+    buf[xh, xl, yh, yl, 0, zh, zl, c] = hid[0]
+    buf[xh, xl, yh, yl, 1, zh, zl, c] = hid[1]
+    sqb[yh, yl, xh, xl, zh, zl, c] = sq[...]
+    sends, sibs = {}, {}
+    for s in range(7):
+        for p in range(7):
+            first = 2 if p == 6 else p
+            if s:
+                sends[p, s - 1].wait_recv()
+            if s < 6:
+                here = cut(p, [(first + k) % 6 for k in range(s)])
+                copy = pltpu.make_async_remote_copy(
+                    src_ref=here, dst_ref=here, send_sem=st_s.at[s, p], recv_sem=st_r.at[s, p],
+                    device_id=partner(x, y, z, c, (first + s) % 6), device_id_type=MESH)
+                copy.start()
+                sends[p, s] = copy
+            here = fresh(p, s)
+            copy = pltpu.make_async_remote_copy(
+                src_ref=here, dst_ref=here, send_sem=sb_s.at[s, p], recv_sem=sb_r.at[s, p],
+                device_id=sib, device_id_type=MESH)
+            copy.start()
+            sibs[p, s] = copy
+    for s in range(7):
+        for p in range(7):
+            sibs[p, s].wait_recv()
+
+    for j in range(4):
+        ax = j if j < 2 else 5 - j
+        for t in range(4):
+            for h in range(2):
+                at = t * 256 + h * 128
+                rows[at:at + 128, :] = buf[j // 2, j % 2, t // 2, t % 2, h].reshape(1792, 128).T
+
+        spot = (yh * 2 + yl) * 256 + (xh * 2 + xl) * 64 + (zh * 2 + zl) * 16
+        own[j] = rows[pl.ds(pl.multiple_of(spot, 16), 16), :]
+        for k, (w, acc) in enumerate(((gate, accg), (up, accu))):
+            v = jnp.concatenate([w[ax, 0], w[ax, 1], w[ax, 3], w[ax, 2]], axis=0)
+            got = jnp.dot(rows[...], v, preferred_element_type=F32)
+            if j:
+                acc[...] += got
+            else:
+                acc[...] = got
+    lane = lax.broadcasted_iota(jnp.int32, (256, 128), 1)
+    token = lax.broadcasted_iota(jnp.int32, (256, 128), 0) // 8
+    for t in range(4):
+        info = sqb[t // 2, t % 2].reshape(32, 8, 128)
+        total = jnp.broadcast_to(jnp.sum(info, axis=0)[None], (32, 8, 128)).reshape(256, 128)
+        total = jnp.sum(jnp.where(lane == token + 32, total, 0.0), axis=1, keepdims=True)
+        mine = (x * 4 + z) * 2 + c
+        wt = jnp.sum(jnp.where(lane == mine, info.reshape(256, 128), 0.0), axis=1, keepdims=True)
+        scale = lax.rsqrt(total / 7168.0 + 1e-6)
+        at = t * 256
+        g = accg[at:at + 256, :] * scale
+        u = accu[at:at + 256, :] * scale
+        act[at:at + 256, :] = (g * u / (1.0 + jnp.exp(-g)) * wt).astype(BF)
+    for s in range(7):
+        for p in range(7):
+            sibs[p, s].wait_send()
+            if s < 6:
+                sends[p, s].wait_send()
+
+
+def moe_in(hid, sq, gate, up, cid):
+    cube = (2,) * 6
+    return pl.pallas_call(
+        moe_in_kernel,
+        out_shape=(jax.ShapeDtypeStruct((1024, 256), BF), jax.ShapeDtypeStruct((4, 16, 1792), BF)),
+        in_specs=[pl.BlockSpec(memory_space=pltpu.VMEM)] * 4,
+        out_specs=(pl.BlockSpec(memory_space=pltpu.VMEM),) * 2,
+        scratch_shapes=[
+            pltpu.VMEM((2, 2, 2, 2, 2, 2, 2, 2, 224, 128), BF),
+            pltpu.VMEM((2, 2, 2, 2, 2, 2, 2, 8, 128), F32),
+            pltpu.VMEM((1024, 1792), BF),
+            pltpu.VMEM((1024, 256), F32),
+            pltpu.VMEM((1024, 256), F32),
+            pltpu.SemaphoreType.DMA((6, 7)), pltpu.SemaphoreType.DMA((6, 7)),
+            pltpu.SemaphoreType.DMA((7, 7)), pltpu.SemaphoreType.DMA((7, 7)),
+        ],
+        compiler_params=pltpu.CompilerParams(collective_id=cid, has_side_effects=True, vmem_limit_bytes=56 << 20),
+        cost_estimate=pl.CostEstimate(flops=2 * 1024 * 512 * 7168, bytes_accessed=1 << 23, transcendentals=0),
+    )(hid, sq, gate.reshape(4, 4, 448, 256), up.reshape(4, 4, 448, 256))
+
+
+def gray_swap(a, axis):
+    parts = [lax.slice_in_dim(a, i, i + 1, axis=axis) for i in (0, 1, 3, 2)]
+    return jnp.concatenate(parts, axis=axis)
 
 
 def per_device(
@@ -78,33 +346,39 @@
     )
     local_width = out_proj.shape[1]
     partial_value = partial_value.astype(jnp.bfloat16).reshape(
-        expert_count, tensor_count, requests, local_width
-    )
-    partial_value = jnp.swapaxes(partial_value, 0, 1).reshape(-1, local_width)
-    summed = lax.psum_scatter(partial_value, "tensor", scatter_dimension=0, tiled=True)
-    summed = summed.reshape(expert_count, requests, local_width)
-    attn_rows = lax.all_to_all(
-        summed, "expert", split_axis=0, concat_axis=2, tiled=True
-    )[0]
-    hidden = residual.astype(jnp.float32) + attn_rows.astype(jnp.float32)
-    normed = hidden * lax.rsqrt(jnp.mean(hidden * hidden, axis=1, keepdims=True) + 1e-06)
-    normed = (normed * norm_gain.astype(jnp.float32)[None, :]).astype(jnp.bfloat16)
-    tokens = lax.all_gather(normed, ("expert", "tensor"), axis=0, tiled=True)
+        4, 4, 2, tensor_count, requests, local_width
+    )
+    partial_value = gray_swap(gray_swap(partial_value, 0), 1)
+    partial_value = jnp.transpose(partial_value, (3, 0, 1, 2, 4, 5)).reshape(-1, local_width)
+    attn_block = lax.psum_scatter(partial_value, "tensor", scatter_dimension=0, tiled=True)
+    residual_block = lax.all_to_all(
+        residual.reshape(requests, expert_count, local_width), "expert", 1, 0, tiled=True
+    ).reshape(4, 4, -1, local_width)
+    residual_block = gray_swap(gray_swap(residual_block, 0), 1).reshape(-1, local_width)
+    hidden = residual_block.astype(F32) + attn_block.astype(F32)
+    squares = jnp.sum(hidden * hidden, axis=1)
+    gain = lax.dynamic_slice_in_dim(
+        norm_gain, lax.axis_index("expert") * local_width, local_width, 0
+    )
+    block = (hidden * gain.astype(F32)[None, :]).astype(BF)
+    block = jnp.swapaxes(block.reshape(2, -1, local_width), 1, 2)
     experts = lax.broadcasted_iota(jnp.int32, (1, 1, expert_count), 2)
     table = jnp.sum(
         jnp.where(routes[:, :, None] == experts, gate_weights[:, :, None], 0.0), axis=1
     )
-    table = lax.all_gather(table, ("expert", "tensor"), axis=0, tiled=True)
-    mine = lax.broadcasted_iota(jnp.int32, (1, expert_count), 1) == lax.axis_index("expert")
-    weight = jnp.sum(jnp.where(mine, table, 0.0), axis=1, keepdims=True)
-    gate_part = jnp.dot(tokens, expert_gate[0], preferred_element_type=jnp.float32)
-    up_part = jnp.dot(tokens, expert_up[0], preferred_element_type=jnp.float32)
-    active = (jax.nn.silu(gate_part) * up_part * weight).astype(jnp.bfloat16)
-    partial_out = jnp.dot(active, expert_down[0], preferred_element_type=jnp.float32)
-    routed_sum = lax.psum_scatter(
-        partial_out.astype(jnp.bfloat16), ("expert", "tensor"), scatter_dimension=0, tiled=True
-    )
-    return (hidden + routed_sum.astype(jnp.float32)).astype(jnp.bfloat16)
+    side = jnp.concatenate(
+        [table, jnp.swapaxes(squares.reshape(expert_count, requests), 0, 1),
+         jnp.zeros((requests, 64), F32)], axis=1)
+    act, own = moe_in(block, side, expert_gate, expert_up, 1)
+    routed = moe_out(act, expert_down[0], 2)
+    core = lax.axis_index("expert") % 2
+    routed = lax.dynamic_slice_in_dim(routed, core * requests, requests, 1)
+    routed = jnp.swapaxes(routed, 0, 1).reshape(requests, -1)
+    own = lax.dynamic_slice_in_dim(own, core * requests, requests, 1)
+    own = gray_swap(gray_swap(own.reshape(4, requests, 4, 448), 0), 2)
+    own = jnp.swapaxes(own, 0, 1).reshape(requests, -1)
+    hidden = own.astype(F32) / norm_gain.astype(F32)[None, :]
+    return (hidden + routed.astype(F32)).astype(BF)
 
 
 def solution(mesh):

time: 930 us -> 278 us (0.30)
  waiting for transfers between devices: 777 us -> 82.2 us
  Pallas kernels: 0 us -> 116 us
  blocking collectives: 72.7 us -> 16 us
  matrix products: 35.7 us -> 15.5 us
    reduce_scatter x1 -> x0, waiting for transfers between devices: 662 us -> none  [per_device(): lax.psum_scatter(partial_out.astype(jnp.bfloat16), ('expert', 'tensor'),...]
    pallas_call x0 -> x2, Pallas kernels: none -> 116 us  [the longest x1 58.9 us: moe_out(): pl.pallas_call(moe_out_kernel, out_shape=jax.ShapeDtypeStruct((2, 16, 358...]
    all_gather x1 -> x0, blocking collectives: 56.7 us -> none  [per_device(): table = lax.all_gather(table, ('expert', 'tensor'), axis=0, tiled=True)]
    dot_general x3 -> x0, matrix products: 20.2 us -> none  [the longest x1 8.88 us: per_device(): jnp.dot(tokens, expert_gate[0], preferred_element_type=jnp.float32)]
    all_gather x1 -> x0, waiting for transfers between devices: 17 us -> none  [per_device(): tokens = lax.all_gather(normed, ('expert', 'tensor'), axis=0, tiled=True)]
    reduce_scatter x1, waiting for transfers between devices: 21.1 us -> 6.58 us  [per_device(): lax.psum_scatter(partial_value, 'tensor', scatter_dimension=0, tiled=True)]
  transfers between devices with their start and end apart: 7 -> 5, of which waited for: 7 -> 5; matrix products, arithmetic and copies ran while one was open for 1% -> 2% of each run, Pallas kernels for 0% -> 0%
where the time goes in v2:
time: 278 us; the launch traced here: 276 us
  Pallas kernels  116 us (42%)
  waiting for transfers between devices  82.2 us (30%)
  blocking collectives  16 us (6%)
  matrix products  15.5 us (6%)
  between operations  13.9 us (5%)
  starting transfers between devices  13.8 us (5%)
  local copies, waits for them, and re-layouts  13.3 us (5%)
  other arithmetic  5.38 us (2%)
    pallas_call x1, Pallas kernels, moe_out(): pl.pallas_call(moe_out_kernel, out_shape=jax.ShapeDtypeStruct((2, 16, 358...  58.9 us
    pallas_call x1, Pallas kernels, moe_in(): pl.pallas_call(moe_in_kernel, out_shape=(jax.ShapeDtypeStruct((1024, 256)...  56.8 us
    all_gather x1, waiting for transfers between devices, per_device(): lax.all_gather(head_out, 'expert', axis=0, tiled=True)  53.5 us
    all_to_all x1, blocking collectives, per_device(): lax.all_to_all(attended, 'tensor', split_axis=1, concat_axis=0, tiled=True)  16 us
    all_to_all x1, waiting for transfers between devices, per_device(): lax.all_to_all(absorbed, 'tensor', split_axis=0, concat_axis=1, tiled=True)  13.2 us
    all_to_all x1, waiting for transfers between devices, per_device(): lax.all_to_all(residual.reshape(requests, expert_count, local_width), 'ex...  7.36 us
    reduce_scatter x1, waiting for transfers between devices, per_device(): lax.psum_scatter(partial_value, 'tensor', scatter_dimension=0, tiled=True)  6.58 us
    dot_general x1, matrix products, per_device(): jnp.dot(lax.all_gather(head_out, 'expert', axis=0, tiled=True), out_proj,...  6 us
  transfers between devices with their start and end apart: 5, of which 5 were waited for; matrix products, arithmetic and copies ran while one was open for 2% of the time, Pallas kernels for 0%

profile of v2, /device:TPU:0, one launch (start us, length us, event | category | flops | bytes accessed | tf_op | source)
XLA Modules:
  0.0 275.7 jit_solution(569974547084961642)
XLA Ops:
  6.5 1.3 reshape.81
  7.8 0.9 reshape.94
  8.8 4.5 %all-to-all-start.2 = ((bf16[4,2,8192]{2,1,0:T(2,128)(2,1)}), bf16[4,2,8192]{2,1,0:T(2,128)(2,1)S(1)}, u32[]{:S(2)}, u32[]{:S(2)}) async-start(bf16[4,2,8192]{2,1,0:T(2,128)(2,1)} %reshape.94), calls=%async_computation.2 | async-start | bytes 262144 | tf_op jit(solution)/shard_map/all_to_all | solution.py:310
  13.3 2.9 %fusion.6 = bf16[32,32,512]{2,0,1:T(8,128)(2,1)S(1)} fusion(bf16[32,128,512]{2,1,0:T(8,128)(2,1)} %param.17, bf16[32,4096]{1,0:T(8,128)(2,1)} %param.15), kind=kOutput, calls=%fused_computation.11 | convolution fusion | flops 134742016 | bytes 5505024 | tf_op jit(solution)/shard_map/rhn,hnl->rhl/dot_general | solution.py:304
  16.3 1.6 copy.100
  17.9 1.4 all-to-all-done.2
  19.3 3.5 %all-to-all-start.1 = ((bf16[32,32,512]{2,1,0:T(8,128)(2,1)}), bf16[32,32,512]{2,1,0:T(8,128)(2,1)S(1)}, u32[]{:S(2)}, u32[]{:S(2)}) async-start(bf16[32,32,512]{2,1,0:T(8,128)(2,1)} %copy.100), calls=%async_computation.1 | async-start | bytes 2097152 | tf_op jit(solution)/shard_map/all_to_all | solution.py:309
  23.9 13.2 %all-to-all-done.1 = bf16[32,32,512]{2,1,0:T(8,128)(2,1)S(1)} async-done(((bf16[32,32,512]{2,1,0:T(8,128)(2,1)}), bf16[32,32,512]{2,1,0:T(8,128)(2,1)S(1)}, u32[]{:S(2)}, u32[]{:S(2)}) %all-to-all-start.1) | async-done | bytes 1048608 | tf_op jit(solution)/shard_map/all_to_all | solution.py:309
  37.2 1.1 copy.101
  38.2 1.6 copy.103
  40.2 3.7 %fusion.2 = (f32[8,128]{1,0:T(8,128)S(1)}, f32[8,128,512]{2,1,0:T(8,128)S(1)}) fusion(pred[8,512]{1,0:T(8,128)(4,1)S(1)} %iota_compare_fusion.7, bf16[8,512,576]{1,2,0:T(8,128)(2,1)} %param.18, bf16[8,128,64]{1,2,0:T(8,128)(2,1)S(1)} %copy.104, bf16[8,128,512]{1,2,0:T(8,128)(2,1)S(1)} %copy.103), kind=kOutput, calls=%fused_computation.6 | convolution fusion | flops 607910912 | bytes 8003584 | tf_op jit(solution)/shard_map/rhc,rpc->rhp/dot_general | solution.py:315
  44.6 1.9 add_convert_fusion
  47.0 16.0 %all_to_all.69 = bf16[8,128,512]{2,0,1:T(8,128)(2,1)S(1)} all-to-all(bf16[8,128,512]{2,0,1:T(8,128)(2,1)S(1)} %copy.106), channel_id=1, replica_groups=mesh['expert'=32,'tensor'=4] {'tensor'}, dimensions={1} | all-to-all | bytes 2097152 | tf_op jit(solution)/shard_map/all_to_all | solution.py:337
  64.6 53.5 %all-gather.2.cloned.1.call-done = bf16[1024,4096]{1,0:T(8,128)(2,1)} async-done(((bf16[32,4096]{1,0:T(8,128)(2,1)}), bf16[1024,4096]{1,0:T(8,128)(2,1)}) %all-gather.2.cloned.1.call-update) | async-done | bytes 8388624 | tf_op jit(solution)/shard_map/all_gather | solution.py:343
  118.1 6.0 %convolution_convert_fusion.1 = bf16[1024,224]{0,1:T(8,128)(2,1)S(1)} fusion(bf16[1024,4096]{1,0:T(8,128)(2,1)} %all-gather.2.cloned.1.call-done, bf16[4096,224]{0,1:T(8,128)(2,1)S(1)} %copy-done), kind=kOutput, calls=%fused_computation.12 | convolution fusion | flops 1879277568 | bytes 10682368 | tf_op jit(solution)/shard_map/dot_general | solution.py:342
  124.9 0.9 copy.113
  126.8 5.6 %all-to-all-start = ((bf16[8,32,224]{2,0,1:T(8,128)(2,1)}), bf16[8,32,224]{2,0,1:T(8,128)(2,1)S(1)}, u32[]{:S(2)}, u32[]{:S(2)}) async-start(bf16[8,32,224]{2,0,1:T(8,128)(2,1)} %copy.98), calls=%async_computation | async-start | bytes 262144 | tf_op jit(solution)/shard_map/all_to_all | solution.py:354
  132.7 7.4 %all-to-all-done = bf16[8,32,224]{2,0,1:T(8,128)(2,1)S(1)} async-done(((bf16[8,32,224]{2,0,1:T(8,128)(2,1)}), bf16[8,32,224]{2,0,1:T(8,128)(2,1)S(1)}, u32[]{:S(2)}, u32[]{:S(2)}) %all-to-all-start) | async-done | bytes 114720 | tf_op jit(solution)/shard_map/all_to_all | solution.py:354
  140.2 6.6 %reduce-scatter.2.cloned.1.call-done = bf16[256,224]{1,0:T(8,128)(2,1)} async-done(((bf16[1024,224]{1,0:T(8,128)(2,1)}), bf16[256,224]{1,0:T(8,128)(2,1)}) %reduce-scatter.2.cloned.1.call-update) | async-done | bytes 114704 | tf_op jit(solution)/shard_map/reduce_scatter | solution.py:353
  146.8 1.0 multiply_reduce_fusion
  149.4 56.8 %shard_map.145 = (bf16[1024,256]{1,0:T(8,128)(2,1)}, bf16[4,16,1792]{2,1,0:T(8,128)(2,1)}) custom-call(bf16[2,224,128]{2,1,0:T(8,128)(2,1)} %bitcast.93, f32[8,128]{1,0:T(8,128)} %maximum_maximum_fusion.sq, bf16[4,4,448,256]{3,2,1,0:T(8,128)(2,1)} %bitcast.100, bf16[4,4,448,256]{3,2,1,0:T(8,128)(2,1)} %bitcast.101), custom_call_target="tpu_custom_call" | custom-call | flops 7516192768 | bytes 8388608 | tf_op jit(solution)/shard_map/pallas_call | solution.py:253
  206.2 0.8 constant_dynamic-slice_fusion.3
  208.3 58.9 %shard_map.146 = bf16[2,16,3584]{2,1,0:T(8,128)(2,1)} custom-call(bf16[2,2,2,2,2,2,16,256]{7,6,5,4,3,2,1,0:T(8,128)(2,1)} %bitcast.103, bf16[256,7168]{1,0:T(8,128)(2,1)} %bitcast.102), custom_call_target="tpu_custom_call" | custom-call | flops 3758096384 | bytes 8388608 | tf_op jit(solution)/shard_map/pallas_call | solution.py:143
  267.2 0.9 dynamic-slice_convert_fusion
  (76 shorter events, 9.6 us)
Async XLA Ops:
  6.5 111.6 %copy-start = (bf16[4096,224]{0,1:T(8,128)(2,1)S(1)}, bf16[4096,224]{0,1:T(8,128)(2,1)}, u32[]{:S(2)}) copy-start(bf16[4096,224]{0,1:T(8,128)(2,1)} %param.22) | copy-start | bytes 5505028
  8.8 10.5 %all-to-all-start.2 = ((bf16[4,2,8192]{2,1,0:T(2,128)(2,1)}), bf16[4,2,8192]{2,1,0:T(2,128)(2,1)S(1)}, u32[]{:S(2)}, u32[]{:S(2)}) async-start(bf16[4,2,8192]{2,1,0:T(2,128)(2,1)} %reshape.94), calls=%async_computation.2 | async-start | bytes 262144 | tf_op jit(solution)/shard_map/all_to_all | solution.py:310
  16.3 6.6 %copy-start.8 = (s32[8]{0:T(128)S(1)}, s32[8]{0:T(128)}, u32[]{:S(2)}) copy-start(s32[8]{0:T(128)} %param.20) | copy-start | bytes 100
  16.3 6.7 %copy-start.5 = (bf16[8,576]{1,0:T(8,128)(2,1)S(1)}, bf16[8,576]{1,0:T(8,128)(2,1)}, u32[]{:S(2)}) copy-start(bf16[8,576]{1,0:T(8,128)(2,1)} %param.19) | copy-start | bytes 27652
  19.3 17.9 %all-to-all-start.1 = ((bf16[32,32,512]{2,1,0:T(8,128)(2,1)}), bf16[32,32,512]{2,1,0:T(8,128)(2,1)S(1)}, u32[]{:S(2)}, u32[]{:S(2)}) async-start(bf16[32,32,512]{2,1,0:T(8,128)(2,1)} %copy.100), calls=%async_computation.1 | async-start | bytes 2097152 | tf_op jit(solution)/shard_map/all_to_all | solution.py:309
  22.8 95.3 %all-gather.2.cloned.1.call-start = ((), (), s32[]{:S(2)}) async-start(), calls=%async_computation.5 | async-start | bytes 8650752 | tf_op jit(solution)/shard_map/all_gather | solution.py:343
  39.9 4.6 %slice-start = ((s8[4718592]{0:T(1024)(128)(4,1)}), s8[4194304]{0:T(1024)(128)(4,1)S(1)}, s32[]{:S(2)}) async-start(s8[4718592]{0:T(1024)(128)(4,1)} %bitcast.98), calls=%async_computation.7 | async-start | bytes 8388608
  40.2 4.4 %slice-start.1 = ((s8[4718592]{0:T(1024)(128)(4,1)}), s8[524288]{0:T(1024)(128)(4,1)S(1)}, s32[]{:S(2)}) async-start(s8[4718592]{0:T(1024)(128)(4,1)} %bitcast.98), calls=%async_computation.8 | async-start | bytes 1048576
  43.8 0.7 copy-start.3
  46.4 16.6 %copy-start.1 = (bf16[32,512,128]{2,1,0:T(8,128)(2,1)S(1)}, bf16[32,512,128]{2,1,0:T(8,128)(2,1)}, u32[]{:S(2)}) copy-start(bf16[32,512,128]{2,1,0:T(8,128)(2,1)} %param.21) | copy-start | bytes 12582916
  64.6 82.2 %reduce-scatter.2.cloned.1.call-start = ((), (), s32[]{:S(2)}) async-start(), calls=%async_computation.6 | async-start | bytes 655360 | tf_op jit(solution)/shard_map/reduce_scatter | solution.py:353
  124.6 1.2 copy-start.2
  124.7 7.7 %copy-start.4 = (bf16[7168]{0:T(1024)(128)(2,1)S(1)}, bf16[7168]{0:T(1024)(128)(2,1)}, u32[]{:S(2)}) copy-start(bf16[7168]{0:T(1024)(128)(2,1)} %param.24) | copy-start | bytes 43012
  124.7 7.8 %copy-start.6 = (f32[8,8]{1,0:T(8,128)S(1)}, f32[8,8]{1,0:T(8,128)}, u32[]{:S(2)}) copy-start(f32[8,8]{1,0:T(8,128)} %param.26) | copy-start | bytes 772
  124.8 7.8 %copy-start.7 = (s32[8,8]{1,0:T(8,128)S(1)}, s32[8,8]{1,0:T(8,128)}, u32[]{:S(2)}) copy-start(s32[8,8]{1,0:T(8,128)} %param.25) | copy-start | bytes 772
  126.8 13.3 %all-to-all-start = ((bf16[8,32,224]{2,0,1:T(8,128)(2,1)}), bf16[8,32,224]{2,0,1:T(8,128)(2,1)S(1)}, u32[]{:S(2)}, u32[]{:S(2)}) async-start(bf16[8,32,224]{2,0,1:T(8,128)(2,1)} %copy.98), calls=%async_computation | async-start | bytes 262144 | tf_op jit(solution)/shard_map/all_to_all | solution.py:354
Sparse Core Ops, SparseCore 0:
  64.7 53.3 all-gather.1
  125.9 20.7 reduce-scatter.1

commit v3 on v2

--- a/solution.py
+++ b/solution.py
@@ -162,12 +162,100 @@
 ROW_N = (80, 80, 64, 80, 80, 64)
 
 
-def moe_in_kernel(hid, sq, gate, up, act, own, buf, sqb, rows, accg, accu, st_s, st_r, sb_s, sb_r):
+def middle_kernel(head, proj, res, gain, table, gate, up, act, own, heads, part, summed, turn, got,
+                  buf, sqb, rows, accg, accu, h_s, h_r, hs_s, hs_r, y_s, y_r, t_s, t_r, st_s, st_r, sb_s, sb_r):
     x, y, z, c = place()
     bits = cube_bits(x, y, z)
     yh, yl, xh, xl, zh, zl = bits
-    meet(range(7), x, y, z, c)
+    across = ((x * 4 + z) * 2 + c, (y + 2) % 4)
+    barrier = pltpu.get_barrier_semaphore()
+    for d in range(7):
+        pl.semaphore_signal(barrier, inc=1, device_id=partner(x, y, z, c, d), device_id_type=MESH)
+    pl.semaphore_signal(barrier, inc=1, device_id=across, device_id_type=MESH)
+    pl.semaphore_wait(barrier, 8)
     sib = partner(x, y, z, c, SIBLING)
+
+    def head_cut(p, free, flip=None):
+        g = lambda d: slice(None) if d in free else (1 - bits[d] if d == flip else bits[d])
+        return heads.at[g(2), g(3), g(4), g(5), c, :, pl.ds(p * 1024, 1024)]
+
+    def around(p, k):
+        return [2 + (p + i) % 4 for i in range(k)]
+
+    def residual_turn(k):
+        d = (SIBLING, 2, 3, 4, 5)[k]
+        mine = c if d == SIBLING else bits[d]
+        at = tuple(1 - mine if e == d else slice(None) for e in (2, 3, 4, 5, SIBLING))
+        copy = pltpu.make_async_remote_copy(
+            src_ref=turn.at[at], dst_ref=got.at[k], send_sem=t_s.at[k], recv_sem=t_r.at[k],
+            device_id=partner(x, y, z, c, d), device_id_type=MESH)
+        copy.start()
+        return copy, at
+
+    heads[xh, xl, zh, zl, c] = head[...]
+    turn[...] = res[...]
+    sends, sibs = {}, {}
+    turning = None
+    for s in range(5):
+        for p in range(4):
+            if s:
+                sends[p, s - 1].wait_recv()
+            if s < 4:
+                here = head_cut(p, around(p, s))
+                copy = pltpu.make_async_remote_copy(
+                    src_ref=here, dst_ref=here, send_sem=h_s.at[s, p], recv_sem=h_r.at[s, p],
+                    device_id=partner(x, y, z, c, 2 + (p + s) % 4), device_id_type=MESH)
+                copy.start()
+                sends[p, s] = copy
+            here = head_cut(p, around(p, s - 1), 2 + (p + s - 1) % 4) if s else head_cut(p, [])
+            copy = pltpu.make_async_remote_copy(
+                src_ref=here, dst_ref=here, send_sem=hs_s.at[s, p], recv_sem=hs_r.at[s, p],
+                device_id=sib, device_id_type=MESH)
+            copy.start()
+            sibs[p, s] = copy
+        if turning is not None:
+            turning[0].wait()
+            turn[turning[1]] = got[s - 1]
+        turning = residual_turn(s)
+    for s in range(5):
+        for p in range(4):
+            sibs[p, s].wait_recv()
+    for k in range(4):
+        v = heads[k // 2, k % 2].reshape(256, 4096)
+        v = jnp.dot(v, proj[...], preferred_element_type=F32).reshape(8, 4, 8, 224)
+        for t in range(4):
+            part[t, k] = v[:, t].reshape(64, 224).astype(BF)
+    copies = []
+    for k in range(1, 4):
+        t = (y + k) % 4
+        copy = pltpu.make_async_remote_copy(
+            src_ref=part.at[t], dst_ref=summed.at[k - 1], send_sem=y_s.at[k - 1], recv_sem=y_r.at[k - 1],
+            device_id=((x * 4 + z) * 2 + c, t), device_id_type=MESH)
+        copy.start()
+        copies.append(copy)
+    turning[0].wait()
+    turn[turning[1]] = got[4]
+    total = part[y].astype(F32)
+    for k in range(3):
+        copies[k].wait_recv()
+        total = total + summed[k].astype(F32)
+    total = total.reshape(256, 224).astype(BF).astype(F32)
+    hidden = total + turn[...].reshape(256, 256)[:, :224]
+    squares = jnp.sum(hidden * hidden, axis=1, keepdims=True).reshape(32, 8, 1)
+    lane3 = lax.broadcasted_iota(jnp.int32, (32, 8, 128), 2)
+    from3 = lax.broadcasted_iota(jnp.int32, (32, 8, 128), 0)
+    spread = jnp.sum(jnp.where(lane3 == from3 + 32, squares, 0.0), axis=0)
+    sqb[yh, yl, xh, xl, zh, zl, c] = table[...] + spread
+    hid = (hidden * gain[...]).T.astype(BF)
+    buf[xh, xl, yh, yl, 0, zh, zl, c] = hid[:, :128]
+    buf[xh, xl, yh, yl, 1, zh, zl, c] = hid[:, 128:]
+    for s in range(5):
+        for p in range(4):
+            sibs[p, s].wait_send()
+            if s < 4:
+                sends[p, s].wait_send()
+    for copy in copies:
+        copy.wait_send()
 
     def cut(p, known):
         g = lambda d: slice(None) if d in known else bits[d]
@@ -186,9 +274,6 @@
             return sqb.at[g(0), g(1), g(2), g(3), g(4), g(5), c]
         return buf.at[g(2), g(3), g(0), g(1), p // 3, g(4), g(5), c, pl.ds(ROW_AT[p], ROW_N[p]), :]
 
-    buf[xh, xl, yh, yl, 0, zh, zl, c] = hid[0]
-    buf[xh, xl, yh, yl, 1, zh, zl, c] = hid[1]
-    sqb[yh, yl, xh, xl, zh, zl, c] = sq[...]
     sends, sibs = {}, {}
     for s in range(7):
         for p in range(7):
@@ -248,25 +333,28 @@
                 sends[p, s].wait_send()
 
 
-def moe_in(hid, sq, gate, up, cid):
-    cube = (2,) * 6
+def middle(head, proj, res, gain, table, gate, up, cid):
+    vm = lambda shape, kind=BF: pltpu.VMEM(shape, kind)
+    dma = lambda *shape: pltpu.SemaphoreType.DMA(shape)
+    two = lambda n: (2,) * n
     return pl.pallas_call(
-        moe_in_kernel,
+        middle_kernel,
         out_shape=(jax.ShapeDtypeStruct((1024, 256), BF), jax.ShapeDtypeStruct((4, 16, 1792), BF)),
-        in_specs=[pl.BlockSpec(memory_space=pltpu.VMEM)] * 4,
+        in_specs=[pl.BlockSpec(memory_space=pltpu.VMEM)] * 7,
         out_specs=(pl.BlockSpec(memory_space=pltpu.VMEM),) * 2,
         scratch_shapes=[
-            pltpu.VMEM((2, 2, 2, 2, 2, 2, 2, 2, 224, 128), BF),
-            pltpu.VMEM((2, 2, 2, 2, 2, 2, 2, 8, 128), F32),
-            pltpu.VMEM((1024, 1792), BF),
-            pltpu.VMEM((1024, 256), F32),
-            pltpu.VMEM((1024, 256), F32),
-            pltpu.SemaphoreType.DMA((6, 7)), pltpu.SemaphoreType.DMA((6, 7)),
-            pltpu.SemaphoreType.DMA((7, 7)), pltpu.SemaphoreType.DMA((7, 7)),
+            vm(two(5) + (32, 4096)), vm((4, 4, 64, 224)), vm((3, 4, 64, 224)),
+            vm(two(5) + (8, 256), F32), vm((5,) + two(4) + (8, 256), F32),
+            vm(two(8) + (224, 128)), vm(two(7) + (8, 128), F32),
+            vm((1024, 1792)), vm((1024, 256), F32), vm((1024, 256), F32),
+            dma(4, 4), dma(4, 4), dma(5, 4), dma(5, 4), dma(3), dma(3), dma(5), dma(5),
+            dma(6, 7), dma(6, 7), dma(7, 7), dma(7, 7),
         ],
-        compiler_params=pltpu.CompilerParams(collective_id=cid, has_side_effects=True, vmem_limit_bytes=56 << 20),
-        cost_estimate=pl.CostEstimate(flops=2 * 1024 * 512 * 7168, bytes_accessed=1 << 23, transcendentals=0),
-    )(hid, sq, gate.reshape(4, 4, 448, 256), up.reshape(4, 4, 448, 256))
+        compiler_params=pltpu.CompilerParams(
+            collective_id=cid, has_side_effects=True, vmem_limit_bytes=60 << 20),
+        cost_estimate=pl.CostEstimate(
+            flops=2 * 1024 * 512 * 7168, bytes_accessed=1 << 23, transcendentals=1 << 18),
+    )(head, proj, res, gain, table, gate.reshape(4, 4, 448, 256), up.reshape(4, 4, 448, 256))
 
 
 def gray_swap(a, axis):
@@ -339,37 +427,23 @@
         "rhl,hlv->rhv", attended, value_absorb, preferred_element_type=jnp.float32
     ).astype(jnp.bfloat16)
     head_out = head_out.reshape(group_rows, -1)
-    partial_value = jnp.dot(
-        lax.all_gather(head_out, "expert", axis=0, tiled=True),
-        out_proj,
-        preferred_element_type=jnp.float32,
-    )
+    requests, model_width = residual.shape
     local_width = out_proj.shape[1]
-    partial_value = partial_value.astype(jnp.bfloat16).reshape(
-        4, 4, 2, tensor_count, requests, local_width
-    )
-    partial_value = gray_swap(gray_swap(partial_value, 0), 1)
-    partial_value = jnp.transpose(partial_value, (3, 0, 1, 2, 4, 5)).reshape(-1, local_width)
-    attn_block = lax.psum_scatter(partial_value, "tensor", scatter_dimension=0, tiled=True)
-    residual_block = lax.all_to_all(
-        residual.reshape(requests, expert_count, local_width), "expert", 1, 0, tiled=True
-    ).reshape(4, 4, -1, local_width)
-    residual_block = gray_swap(gray_swap(residual_block, 0), 1).reshape(-1, local_width)
-    hidden = residual_block.astype(F32) + attn_block.astype(F32)
-    squares = jnp.sum(hidden * hidden, axis=1)
+    blocks = jnp.pad(
+        jnp.swapaxes(residual.reshape(requests, -1, local_width), 0, 1).astype(F32),
+        ((0, 0), (0, 0), (0, 256 - local_width)),
+    )
+    blocks = gray_swap(gray_swap(blocks.reshape(4, 4, 2, requests, 256), 0), 1)
+    blocks = blocks.reshape(2, 2, 2, 2, 2, requests, 256)
     gain = lax.dynamic_slice_in_dim(
         norm_gain, lax.axis_index("expert") * local_width, local_width, 0
     )
-    block = (hidden * gain.astype(F32)[None, :]).astype(BF)
-    block = jnp.swapaxes(block.reshape(2, -1, local_width), 1, 2)
-    experts = lax.broadcasted_iota(jnp.int32, (1, 1, expert_count), 2)
+    gain = gain.astype(F32)[None, :]
+    experts = lax.broadcasted_iota(jnp.int32, (1, 1, 128), 2)
     table = jnp.sum(
         jnp.where(routes[:, :, None] == experts, gate_weights[:, :, None], 0.0), axis=1
     )
-    side = jnp.concatenate(
-        [table, jnp.swapaxes(squares.reshape(expert_count, requests), 0, 1),
-         jnp.zeros((requests, 64), F32)], axis=1)
-    act, own = moe_in(block, side, expert_gate, expert_up, 1)
+    act, own = middle(head_out, out_proj, blocks, gain, table, expert_gate, expert_up, 1)
     routed = moe_out(act, expert_down[0], 2)
     core = lax.axis_index("expert") % 2
     routed = lax.dynamic_slice_in_dim(routed, core * requests, requests, 1)

time: 278 us -> 226 us (0.81)
  waiting for transfers between devices: 82.2 us -> 22.9 us
  Pallas kernels: 116 us -> 160 us
  blocking collectives: 16 us -> 0 us
  between operations: 13.9 us -> 0.37 us
  matrix products: 15.5 us -> 11.6 us
    all_gather x1 -> x0, waiting for transfers between devices: 53.5 us -> none  [per_device(): lax.all_gather(head_out, 'expert', axis=0, tiled=True)]
    pallas_call x1, Pallas kernels: 56.8 us -> 103 us  [middle(): pl.pallas_call(middle_kernel, out_shape=(jax.ShapeDtypeStruct((1024, 256)...]
    all_to_all x1 -> x0, blocking collectives: 16 us -> none  [per_device(): lax.all_to_all(attended, 'tensor', split_axis=1, concat_axis=0, tiled=True)]
    reduce_scatter x1 -> x0, waiting for transfers between devices: 6.58 us -> none  [per_device(): lax.psum_scatter(partial_value, 'tensor', scatter_dimension=0, tiled=True)]
    dot_general x1 -> x0, matrix products: 6 us -> none  [per_device(): jnp.dot(lax.all_gather(head_out, 'expert', axis=0, tiled=True), out_proj,...]
  transfers between devices with their start and end apart: 5 -> 3, of which waited for: 5 -> 3; matrix products, arithmetic and copies ran while one was open for 2% -> 5% of each run, Pallas kernels for 0% -> 0%
where the time goes in v3:
time: 226 us; the launch traced here: 224 us
  Pallas kernels  160 us (71%)
  waiting for transfers between devices  22.9 us (10%)
  local copies, waits for them, and re-layouts  11.9 us (5%)
  starting transfers between devices  11.7 us (5%)
  matrix products  11.6 us (5%)
  other arithmetic  5.41 us (2%)
    pallas_call x1, Pallas kernels, middle(): pl.pallas_call(middle_kernel, out_shape=(jax.ShapeDtypeStruct((1024, 256)...  103 us
    pallas_call x1, Pallas kernels, moe_out(): pl.pallas_call(moe_out_kernel, out_shape=jax.ShapeDtypeStruct((2, 16, 358...  57.6 us
    all_to_all x1, waiting for transfers between devices, per_device(): lax.all_to_all(absorbed, 'tensor', split_axis=0, concat_axis=1, tiled=True)  13.6 us
    all_to_all x1, waiting for transfers between devices, per_device(): lax.all_to_all(attended, 'tensor', split_axis=1, concat_axis=0, tiled=True)  7.83 us
    all_to_all x1, starting transfers between devices, per_device(): lax.all_to_all(rope_query, 'tensor', split_axis=0, concat_axis=1, tiled=T...  4.55 us
  transfers between devices with their start and end apart: 3, of which 3 were waited for; matrix products, arithmetic and copies ran while one was open for 5% of the time, Pallas kernels for 0%

profile of v3, /device:TPU:0, one launch (start us, length us, event | category | flops | bytes accessed | tf_op | source)
XLA Modules:
  0.0 224.1 jit_solution(12723459603512342962)
XLA Ops:
  0.0 1.2 reshape.64
  1.2 0.9 reshape.75
  2.1 4.5 %all-to-all-start.1 = ((bf16[4,2,8192]{2,1,0:T(2,128)(2,1)}), bf16[4,2,8192]{2,1,0:T(2,128)(2,1)S(1)}, u32[]{:S(2)}, u32[]{:S(2)}) async-start(bf16[4,2,8192]{2,1,0:T(2,128)(2,1)} %reshape.75), calls=%async_computation.1 | async-start | bytes 262144 | tf_op jit(solution)/shard_map/all_to_all | solution.py:398
  6.7 2.9 %fusion.6 = bf16[32,32,512]{2,0,1:T(8,128)(2,1)S(1)} fusion(bf16[32,128,512]{2,1,0:T(8,128)(2,1)} %param.17, bf16[32,4096]{1,0:T(8,128)(2,1)S(1)} %copy-done), kind=kOutput, calls=%fused_computation.9 | convolution fusion | flops 134742016 | bytes 5505024 | tf_op jit(solution)/shard_map/rhn,hnl->rhl/dot_general | solution.py:392
  9.6 1.6 copy.73
  11.1 1.5 all-to-all-done.1
  12.6 3.5 %all-to-all-start = ((bf16[32,32,512]{2,1,0:T(8,128)(2,1)}), bf16[32,32,512]{2,1,0:T(8,128)(2,1)S(1)}, u32[]{:S(2)}, u32[]{:S(2)}) async-start(bf16[32,32,512]{2,1,0:T(8,128)(2,1)} %copy.73), calls=%async_computation | async-start | bytes 2097152 | tf_op jit(solution)/shard_map/all_to_all | solution.py:397
  16.9 13.6 %all-to-all-done = bf16[32,32,512]{2,1,0:T(8,128)(2,1)S(1)} async-done(((bf16[32,32,512]{2,1,0:T(8,128)(2,1)}), bf16[32,32,512]{2,1,0:T(8,128)(2,1)S(1)}, u32[]{:S(2)}, u32[]{:S(2)}) %all-to-all-start) | async-done | bytes 1048608 | tf_op jit(solution)/shard_map/all_to_all | solution.py:397
  31.5 3.7 %fusion.2 = (f32[8,128]{1,0:T(8,128)S(1)}, f32[8,128,512]{2,1,0:T(8,128)S(1)}) fusion(pred[8,512]{1,0:T(8,128)(4,1)S(1)} %iota_compare_fusion.4, bf16[8,512,576]{1,2,0:T(8,128)(2,1)} %param.18, bf16[8,128,64]{1,2,0:T(8,128)(2,1)S(1)} %copy.77, bf16[8,128,512]{1,2,0:T(8,128)(2,1)S(1)} %copy.76), kind=kOutput, calls=%fused_computation.6 | convolution fusion | flops 607910912 | bytes 8003584 | tf_op jit(solution)/shard_map/rhc,rpc->rhp/dot_general | solution.py:403
  35.9 1.9 add_convert_fusion
  37.8 1.5 copy.79
  39.3 3.6 %all-to-all-start.2 = ((bf16[8,128,512]{2,0,1:T(8,128)(2,1)}), bf16[8,128,512]{2,0,1:T(8,128)(2,1)S(1)}, u32[]{:S(2)}, u32[]{:S(2)}) async-start(bf16[8,128,512]{2,0,1:T(8,128)(2,1)} %copy.79), calls=%async_computation.2 | async-start | bytes 2097152 | tf_op jit(solution)/shard_map/all_to_all | solution.py:425
  43.2 2.5 %copy.86.proj = bf16[4096,224]{1,0:T(8,128)(2,1)} copy(bf16[4096,224]{0,1:T(8,128)(2,1)S(1)} %copy-done.1) | data formatting | bytes 3670016 | tf_op args[7]
  45.7 0.7 dynamic-slice_convert_fusion.1
  46.4 1.4 select_reduce_fusion.table
  47.8 0.7 fusion.19
  48.5 7.8 %all-to-all-done.2 = bf16[8,128,512]{2,0,1:T(8,128)(2,1)S(1)} async-done(((bf16[8,128,512]{2,0,1:T(8,128)(2,1)}), bf16[8,128,512]{2,0,1:T(8,128)(2,1)S(1)}, u32[]{:S(2)}, u32[]{:S(2)}) %all-to-all-start.2) | async-done | bytes 1048608 | tf_op jit(solution)/shard_map/all_to_all | solution.py:425
  56.4 2.9 %fusion.7 = bf16[32,4,8,128]{3,2,1,0:T(8,128)(2,1)S(1)} fusion(bf16[32,512,128]{2,1,0:T(8,128)(2,1)} %param.21, bf16[8,4,32,512]{3,0,2,1:T(8,128)(2,1)S(1)} %bitcast.53), kind=kOutput, calls=%fused_computation.12 | convolution fusion | flops 134348800 | bytes 5505024 | tf_op jit(solution)/shard_map/rhl,hlv->rhv/dot_general | solution.py:426
  59.3 0.8 copy.104
  60.0 102.6 %shard_map.145 = (bf16[1024,256]{1,0:T(8,128)(2,1)}, bf16[4,16,1792]{2,1,0:T(8,128)(2,1)}) custom-call(bf16[32,4096]{1,0:T(8,128)(2,1)} %bitcast.67, bf16[4096,224]{1,0:T(8,128)(2,1)} %copy.86.proj, f32[2,2,2,2,2,8,256]{6,5,4,3,2,1,0:T(8,128)} %bitcast.66, f32[1,224]{1,0:T(1,128)} %bitcast.71, f32[8,128]{1,0:T(8,128)} %select_reduce_fusion.table, ...), custom_call_target="tpu_custom_call" | custom-call | flops 7516192768 | bytes 8388608 | tf_op jit(solution)/shard_map/pallas_call | solution.py:340
  162.6 0.8 constant_dynamic-slice_fusion.3
  164.9 57.6 %shard_map.146 = bf16[2,16,3584]{2,1,0:T(8,128)(2,1)} custom-call(bf16[2,2,2,2,2,2,16,256]{7,6,5,4,3,2,1,0:T(8,128)(2,1)} %bitcast.77, bf16[256,7168]{1,0:T(8,128)(2,1)} %bitcast.76), custom_call_target="tpu_custom_call" | custom-call | flops 3758096384 | bytes 8388608 | tf_op jit(solution)/shard_map/pallas_call | solution.py:143
  222.5 0.9 dynamic-slice_convert_fusion
  223.4 0.7 add_convert_fusion.1
  (51 shorter events, 4.0 us)
Async XLA Ops:
  0.0 6.7 %copy-start = (bf16[32,4096]{1,0:T(8,128)(2,1)S(1)}, bf16[32,4096]{1,0:T(8,128)(2,1)}, u32[]{:S(2)}) copy-start(bf16[32,4096]{1,0:T(8,128)(2,1)} %param.15) | copy-start | bytes 786436
  2.1 10.5 %all-to-all-start.1 = ((bf16[4,2,8192]{2,1,0:T(2,128)(2,1)}), bf16[4,2,8192]{2,1,0:T(2,128)(2,1)S(1)}, u32[]{:S(2)}, u32[]{:S(2)}) async-start(bf16[4,2,8192]{2,1,0:T(2,128)(2,1)} %reshape.75), calls=%async_computation.1 | async-start | bytes 262144 | tf_op jit(solution)/shard_map/all_to_all | solution.py:398
  9.5 6.7 %copy-start.2 = (bf16[8,7168]{1,0:T(8,128)(2,1)S(1)}, bf16[8,7168]{1,0:T(8,128)(2,1)}, u32[]{:S(2)}) copy-start(bf16[8,7168]{1,0:T(8,128)(2,1)} %param.23) | copy-start | bytes 344068
  9.5 6.9 %copy-start.5 = (s32[8]{0:T(128)S(1)}, s32[8]{0:T(128)}, u32[]{:S(2)}) copy-start(s32[8]{0:T(128)} %param.20) | copy-start | bytes 100
  9.6 6.9 %copy-start.4 = (bf16[8,576]{1,0:T(8,128)(2,1)S(1)}, bf16[8,576]{1,0:T(8,128)(2,1)}, u32[]{:S(2)}) copy-start(bf16[8,576]{1,0:T(8,128)(2,1)} %param.19) | copy-start | bytes 27652
  12.6 17.8 %all-to-all-start = ((bf16[32,32,512]{2,1,0:T(8,128)(2,1)}), bf16[32,32,512]{2,1,0:T(8,128)(2,1)S(1)}, u32[]{:S(2)}, u32[]{:S(2)}) async-start(bf16[32,32,512]{2,1,0:T(8,128)(2,1)} %copy.73), calls=%async_computation | async-start | bytes 2097152 | tf_op jit(solution)/shard_map/all_to_all | solution.py:397
  31.2 4.6 %slice-start = ((s8[4718592]{0:T(1024)(128)(4,1)}), s8[4194304]{0:T(1024)(128)(4,1)S(1)}, s32[]{:S(2)}) async-start(s8[4718592]{0:T(1024)(128)(4,1)} %bitcast.72), calls=%async_computation.3 | async-start | bytes 8388608
  31.5 4.4 %slice-start.1 = ((s8[4718592]{0:T(1024)(128)(4,1)}), s8[524288]{0:T(1024)(128)(4,1)S(1)}, s32[]{:S(2)}) async-start(s8[4718592]{0:T(1024)(128)(4,1)} %bitcast.72), calls=%async_computation.4 | async-start | bytes 1048576
  39.3 3.9 %copy-start.1 = (bf16[4096,224]{0,1:T(8,128)(2,1)S(1)}, bf16[4096,224]{0,1:T(8,128)(2,1)}, u32[]{:S(2)}) copy-start(bf16[4096,224]{0,1:T(8,128)(2,1)} %param.22) | copy-start | bytes 5505028
  39.3 17.0 %all-to-all-start.2 = ((bf16[8,128,512]{2,0,1:T(8,128)(2,1)}), bf16[8,128,512]{2,0,1:T(8,128)(2,1)S(1)}, u32[]{:S(2)}, u32[]{:S(2)}) async-start(bf16[8,128,512]{2,0,1:T(8,128)(2,1)} %copy.79), calls=%async_computation.2 | async-start | bytes 2097152 | tf_op jit(solution)/shard_map/all_to_all | solution.py:425
  43.2 2.5 %copy-start.3 = (bf16[7168]{0:T(1024)(128)(2,1)S(1)}, bf16[7168]{0:T(1024)(128)(2,1)}, u32[]{:S(2)}) copy-start(bf16[7168]{0:T(1024)(128)(2,1)} %param.24) | copy-start | bytes 43012

commit v4 on v1

v4 whole, which is shorter than its diff:
```python
import functools, math
import jax, jax.numpy as jnp
from jax import lax
from jax.experimental import pallas as pl
from jax.experimental.pallas import tpu as pltpu
from jax.sharding import PartitionSpec as P

MESH = pl.DeviceIdType.MESH
BF = jnp.bfloat16
F32 = jnp.float32
SIBLING = 6


def place():
    e, y = lax.axis_index("expert"), lax.axis_index("tensor")
    return e // 8, y, (e // 2) % 4, e % 2


def cube_bits(x, y, z):
    out = []
    for v in (y, x, z):
        g = jnp.where(v >= 2, 5 - v, v)
        out += [g // 2, g % 2]
    return out


def partner(x, y, z, c, d):
    if d == SIBLING:
        return ((x * 4 + z) * 2 + 1 - c, y)
    at = [y, x, z]
    v = at[d // 2]
    at[d // 2] = 3 - v if d % 2 == 0 else v + 1 - 2 * (v % 2)
    y, x, z = at
    return ((x * 4 + z) * 2 + c, y)


def meet(dims, x, y, z, c):
    barrier = pltpu.get_barrier_semaphore()
    for d in dims:
        pl.semaphore_signal(barrier, inc=1, device_id=partner(x, y, z, c, d), device_id_type=MESH)
    pl.semaphore_wait(barrier, len(dims))


FREE, OTHER, MINE = "free", "other", "mine"


def index_of(bits, spec):
    return [slice(None) if spec.get(d) == FREE else (1 - bits[d] if spec.get(d) == OTHER else bits[d])
            for d in range(6)]


class Gather:
    def __init__(self, order, cut, send_sem, recv_sem, where, split=True):
        self.order, self.cut, self.where, self.split = order, cut, where, split
        self.sems = send_sem, recv_sem
        self.copies = {}

    def send(self, s, part):
        o = self.order
        spec = {d: FREE for d in o[:max(s - 1, 0) if self.split else s]}
        if part:
            spec[o[s - 1]] = OTHER
        ref = self.cut(spec)
        copy = pltpu.make_async_remote_copy(
            src_ref=ref, dst_ref=ref, send_sem=self.sems[0].at[s, part], recv_sem=self.sems[1].at[s, part],
            device_id=partner(*self.where, o[s]), device_id_type=MESH)
        copy.start()
        self.copies[s, part] = copy

    def last(self, part):
        o = self.order
        spec = {d: FREE for d in o[:-2]}
        spec[o[-1]] = OTHER
        if part:
            spec[o[-2]] = OTHER
        return spec

    def turn(self, s):
        if s == 0:
            self.send(0, 0)
            if self.split:
                self.send(1, 0)
            return
        for part in (0, 1) if self.split and s > 1 else (0,):
            self.copies[s - 1, part].wait_recv()
        if s < len(self.order):
            if self.split:
                self.send(s, 1)
                if s + 1 < len(self.order):
                    self.send(s + 1, 0)
            else:
                self.send(s, 0)

    def finish(self, part):
        self.copies[len(self.order) - 1, part].wait_recv()

    def wait_sends(self):
        for copy in self.copies.values():
            copy.wait_send()


ROW_AT = (0, 80, 160, 240, 320, 384)
ROW_N = (80, 80, 80, 80, 64, 64)


def middle_kernel(head, proj_hbm, proj2_hbm, res, gains, routes, weights, gate_hbm, up_hbm, gate2_hbm, up2_hbm,
                  act, own, proj, wts, heads, part, summed, gainf, turn, got, buf, sqb, acc, loads,
                  h_s, h_r, y_s, y_r, t_s, t_r, st_s, st_r):
    x, y, z, c = where = place()
    bits = cube_bits(x, y, z)
    yh, yl, xh, xl, zh, zl = bits
    chip = (x * 4 + z) * 2
    across = (chip + c, (y + 2) % 4)
    fetch = [pltpu.make_async_copy(a, b, loads.at[n]) for n, (a, b) in enumerate((
        (proj_hbm, proj.at[c]), (proj2_hbm, proj.at[1 - c]), (gate_hbm, wts.at[0, 0]), (up_hbm, wts.at[0, 1]),
        (gate2_hbm, wts.at[1, 0]), (up2_hbm, wts.at[1, 1])))]
    for copy in fetch:
        copy.start()
    barrier = pltpu.get_barrier_semaphore()
    for d in range(6):
        pl.semaphore_signal(barrier, inc=1, device_id=partner(x, y, z, c, d), device_id_type=MESH)
    pl.semaphore_signal(barrier, inc=1, device_id=across, device_id_type=MESH)
    heads[xh, xl, zh, zl] = head[...]
    for k in range(16):
        sx, sz = k // 4 ^ k // 8, k % 4 ^ k % 4 // 2
        v = [res[:, e * 224:(e + 1) * 224].astype(F32) for e in (2 * k, 2 * k + 1)]
        turn[sx // 2, sx % 2, sz // 2, sz % 2] = jnp.concatenate(v, axis=0).astype(BF)
    gainf[...] = gains[...].astype(F32)
    lane = lax.broadcasted_iota(jnp.int32, (8, 128), 1)
    table = jnp.zeros((8, 128), F32)
    for k in range(8):
        table = table + jnp.where(lane == routes[:, k:k + 1], weights[:, k:k + 1], 0.0)
    acc[...] = jnp.zeros_like(acc)
    pl.semaphore_wait(barrier, 7)

    def head_cut(p):
        def cut(spec):
            g = index_of(bits, spec)
            return heads.at[g[2], g[3], g[4], g[5], :, pl.ds(p * 1024, 1024)]
        return cut

    first = [Gather([2 + (p + i) % 4 for i in range(4)], head_cut(p), h_s.at[p], h_r.at[p], where) for p in range(4)]

    def residual_turn(k):
        d = 2 + k
        at = tuple(1 - bits[d] if e == d else slice(None) for e in (2, 3, 4, 5))
        copy = pltpu.make_async_remote_copy(
            src_ref=turn.at[at], dst_ref=got.at[k], send_sem=t_s.at[k], recv_sem=t_r.at[k],
            device_id=partner(x, y, z, c, d), device_id_type=MESH)
        copy.start()
        return copy, at

    turning = None
    for s in range(4):
        for g in first:
            g.turn(s)
        if turning is not None:
            turning[0].wait()
            turn[turning[1]] = got[s - 1]
        turning = residual_turn(s)
    for copy in fetch[:2]:
        copy.wait()
    for half in range(2):
        for g in first:
            g.finish(half)
    for k in range(2):
        v = heads[k].reshape(256, 4096)
        for n in range(2):
            o = lax.dot_general(v, proj[n], (((1,), (1,)), ((), ())), preferred_element_type=F32)
            o = o.reshape(8, 4, 8, 224)
            for t in range(4):
                part[t, n, k] = o[:, t].reshape(64, 224).astype(BF)
    copies = []
    for k in range(1, 4):
        t = (y + k) % 4
        copy = pltpu.make_async_remote_copy(
            src_ref=part.at[t], dst_ref=summed.at[k - 1], send_sem=y_s.at[k - 1], recv_sem=y_r.at[k - 1],
            device_id=(chip + c, t), device_id_type=MESH)
        copy.start()
        copies.append(copy)
    turning[0].wait()
    turn[turning[1]] = got[3]
    total = part[y].astype(F32)
    for k in range(3):
        copies[k].wait_recv()
        total = total + summed[k].astype(F32)
    total = total.astype(BF).astype(F32).reshape(2, 128, 224)
    residual = turn[...].astype(F32).reshape(16, 2, 8, 224)
    squares, hid = 0.0, []
    for n in range(2):
        hidden = total[n] + residual[:, n].reshape(128, 224)
        squares = squares + jnp.sum(hidden * hidden, axis=1, keepdims=True)
        hid.append((hidden * gainf[pl.ds(chip + n, 1), :]).T)
    lane3 = lax.broadcasted_iota(jnp.int32, (16, 8, 128), 2)
    from3 = lax.broadcasted_iota(jnp.int32, (16, 8, 128), 0)
    spread = jnp.sum(jnp.where(lane3 == from3 + 32, squares.reshape(16, 8, 1), 0.0), axis=0)
    sqb[yh, yl, xh, xl, zh, zl] = table + spread
    buf[xh, xl, yh, yl, zh, zl] = jnp.concatenate(hid, axis=0).astype(BF)

    def cut_of(p):
        def cut(spec):
            g = index_of(bits, spec)
            if p == 6:
                return sqb.at[g[0], g[1], g[2], g[3], g[4], g[5]]
            return buf.at[g[2], g[3], g[0], g[1], g[4], g[5], pl.ds(ROW_AT[p], ROW_N[p]), :]
        return cut

    def order_of(p):
        return [((4 if p == 6 else p) + k) % 6 for k in range(6)]

    second = [Gather(order_of(p), cut_of(p), st_s.at[p], st_r.at[p], where, p < 6) for p in range(7)]

    def work(p, spec):
        rows = pl.ds(ROW_AT[p], ROW_N[p])
        opts = [(0, 1) if spec.get(d) == FREE else ((1 - bits[d],) if spec.get(d) == OTHER else (bits[d],))
                for d in range(6)]
        inner = [(i, j, k, l) for i in opts[2] for j in opts[3] for k in opts[4] for l in opts[5]]
        outer = [(a, b) for a in opts[0] for b in opts[1]]
        lhs = []
        for a, b in outer:
            slab = [buf[i, j, a, b, k, l, rows, :] for i, j, k, l in inner]
            lhs.append(jnp.concatenate(slab, axis=0).T)
        lhs = jnp.concatenate(lhs, axis=0)
        for n in range(2):
            for m in range(2):
                v = [wts[n, m, 2 * i + (i + j - 2 * i * j), 2 * k + (k + l - 2 * k * l), rows, :]
                     for i, j, k, l in inner]
                o = jnp.dot(lhs, jnp.concatenate(v, axis=0), preferred_element_type=F32)
                for q, (a, b) in enumerate(outer):
                    acc[n, m, a, b] += o[q * 128:(q + 1) * 128]

    for s in range(6):
        for g in second:
            g.turn(s)
    for copy in fetch[2:]:
        copy.wait()
    for p in range(6):
        work(p, {d: FREE for d in order_of(p)[:5]})
    second[6].turn(6)
    for half in range(2):
        for p in range(6):
            second[p].finish(half)
            work(p, second[p].last(half))

    lane = lax.broadcasted_iota(jnp.int32, (128, 128), 1)
    token = lax.broadcasted_iota(jnp.int32, (128, 128), 0) // 8
    for t in range(4):
        info = sqb[t // 2, t % 2].reshape(16, 8, 128)
        total = jnp.broadcast_to(jnp.sum(info, axis=0)[None], (16, 8, 128)).reshape(128, 128)
        total = jnp.sum(jnp.where(lane == token + 32, total, 0.0), axis=1, keepdims=True)
        scale = lax.rsqrt(total / 7168.0 + 1e-6)
        for n in range(2):
            expert = chip + (c if n == 0 else 1 - c)
            wt = jnp.sum(jnp.where(lane == expert, info.reshape(128, 128), 0.0), axis=1, keepdims=True)
            g = acc[n, 0, t // 2, t % 2] * scale
            u = acc[n, 1, t // 2, t % 2] * scale
            act[t * 128:(t + 1) * 128, n * 256:(n + 1) * 256] = g * u / (1.0 + jnp.exp(-g)) * wt
    spot = (xh * 2 + xl) * 32 + (zh * 2 + zl) * 8
    row = lax.broadcasted_iota(jnp.int32, (16, 128), 0)
    pick = (lax.broadcasted_iota(jnp.int32, (16, 128), 1) == row + spot) & (row < 8)
    pick = jnp.where(pick, 1.0, 0.0).astype(BF)
    for j in range(4):
        v = jnp.concatenate([buf[j // 2, j % 2, yh, yl, k // 2, k % 2] for k in (0, 1, 3, 2)], axis=0)
        v = lax.dot_general(pick, v, (((1,), (1,)), ((), ())), preferred_element_type=F32)
        ax = j if j < 2 else 5 - j
        own[:, ax * 1792:(ax + 1) * 1792] = v.astype(BF)
    for g in first + second:
        g.wait_sends()
    for copy in copies:
        copy.wait_send()


def middle(head, proj, proj2, res, gains, routes, weights, gates, cid):
    vm = lambda shape, kind=BF: pltpu.VMEM(shape, kind)
    dma = lambda *shape: pltpu.SemaphoreType.DMA(shape)
    two = lambda n: (2,) * n
    inside = pl.BlockSpec(memory_space=pltpu.VMEM)
    outside = pl.BlockSpec(memory_space=pl.ANY)
    return pl.pallas_call(
        middle_kernel,
        out_shape=(jax.ShapeDtypeStruct((512, 512), F32), jax.ShapeDtypeStruct((16, 7168), BF)),
        in_specs=[inside, outside, outside] + [inside] * 4 + [outside] * 4,
        out_specs=(inside, inside),
        scratch_shapes=[
            vm((2, 224, 4096)), vm((2, 2, 4, 4, 448, 256)),
            vm(two(4) + (32, 4096)), vm((4, 2, 2, 64, 224)), vm((3, 2, 2, 64, 224)),
            vm((32, 224), F32), vm(two(4) + (16, 224)), vm((4,) + two(3) + (16, 224)),
            vm(two(6) + (448, 128)), vm(two(6) + (8, 128), F32), vm((2, 2, 2, 2, 128, 256), F32),
            dma(6), dma(4, 4, 2), dma(4, 4, 2), dma(3), dma(3), dma(4), dma(4), dma(7, 6, 2), dma(7, 6, 2),
        ],
        compiler_params=pltpu.CompilerParams(
            collective_id=cid, has_side_effects=True, vmem_limit_bytes=56 << 20),
        cost_estimate=pl.CostEstimate(
            flops=2 * 1024 * 512 * 7168, bytes_accessed=1 << 23, transcendentals=1 << 18),
    )(head, proj, proj2, res, gains, routes, weights, *[g.reshape(4, 4, 448, 256) for g in gates])


OUT_W = (640, 640, 640, 640, 512, 512)
OUT_AT = (0, 640, 1280, 1920, 2560, 3072)


def moe_out_kernel(act, down_hbm, others_hbm, out, down, ps, r0, r1, r2, r3, r4, r5, loads, st_s, st_r):
    x, y, z, c = place()
    bits = cube_bits(x, y, z)
    rs = (r0, r1, r2, r3, r4, r5)
    fetch = [
        pltpu.make_async_copy(down_hbm, down.at[pl.ds(0, 256)], loads.at[0]),
        pltpu.make_async_copy(others_hbm, down.at[pl.ds(256, 256)], loads.at[1]),
    ]
    for copy in fetch:
        copy.start()
    meet(range(6), x, y, z, c)

    def cut(ref, p, spec):
        idx = tuple(bits[d] if spec[d] == MINE else (1 - bits[d] if spec[d] == OTHER else slice(None))
                    for d in range(6) if d in spec)
        return ref.at[idx + (slice(None), pl.ds(OUT_AT[p], OUT_W[p]))]

    def spec_of(p, s, which):
        spec = {d: FREE for d in range(6)}
        for k in range(s):
            spec[(p + k) % 6] = MINE
        spec[(p + s) % 6] = OTHER
        if s < 5:
            spec[(p + s + 1) % 6] = OTHER if which == 0 else MINE
        return spec

    def product(p, spec):
        rows = act[tuple(bits[d] if spec[d] == MINE else (1 - bits[d] if spec[d] == OTHER else slice(None))
                         for d in range(6))]
        free = sum(spec[d] == FREE for d in range(6))
        rows = rows.reshape(8 << free, 512).astype(BF)
        halves = []
        for at in (OUT_AT[p], 3584 + OUT_AT[p]):
            o = jnp.dot(rows, down[:, at:at + OUT_W[p]], preferred_element_type=F32)
            halves.append(o.reshape(1 << free, 8, OUT_W[p]))
        got = jnp.concatenate(halves, axis=1).astype(BF)
        cut(ps, p, spec)[...] = got.reshape((2,) * free + (16, OUT_W[p]))

    sends = {}

    def landing(p, s, which):
        spec = spec_of(p, s, which)
        return cut(rs[s], p, {d: spec[d] for d in range(6) if d not in [(p + k) % 6 for k in range(s + 1)]})

    def send(p, s, which):
        copy = pltpu.make_async_remote_copy(
            src_ref=cut(ps, p, spec_of(p, s, which)), dst_ref=landing(p, s, which),
            send_sem=st_s.at[s, p, which], recv_sem=st_r.at[s, p, which],
            device_id=partner(x, y, z, c, (p + s) % 6), device_id_type=MESH)
        copy.start()
        sends[p, s, which] = copy

    def take(p, s, which):
        sends[p, s, which].wait_recv()
        spec = dict(spec_of(p, s, which))
        spec[(p + s) % 6] = MINE
        here, other = cut(ps, p, spec), landing(p, s, which)
        here[...] = (here[...].astype(F32) + other[...].astype(F32)).astype(BF)

    for copy in fetch:
        copy.wait()
    for which in (0, 1):
        for p in range(6):
            product(p, spec_of(p, 0, which))
            send(p, 0, which)
    for p in range(6):
        product(p, {d: MINE if d == p else FREE for d in range(6)})
    for s in range(5):
        for p in range(6):
            take(p, s, 0)
            send(p, s + 1, 0)
            if s < 4:
                send(p, s + 1, 1)
        for p in range(6):
            take(p, s, 1)
    for p in range(6):
        take(p, 5, 0)
    mine = ps[tuple(bits)].astype(F32)
    out[:, :3584] = mine[:8]
    out[:, 3584:] = mine[8:]
    for copy in sends.values():
        copy.wait_send()


def moe_out(act, down, others, cid):
    cube = (2,) * 6
    dma = lambda *shape: pltpu.SemaphoreType.DMA(shape)
    inside = pl.BlockSpec(memory_space=pltpu.VMEM)
    outside = pl.BlockSpec(memory_space=pl.ANY)
    return pl.pallas_call(
        moe_out_kernel,
        out_shape=jax.ShapeDtypeStruct((8, 7168), F32),
        in_specs=[inside, outside, outside],
        out_specs=inside,
        scratch_shapes=[
            pltpu.VMEM((512, 7168), BF),
            pltpu.VMEM(cube + (16, 3584), BF),
        ] + [pltpu.VMEM((2,) * (5 - s) + (16, 3584), BF) for s in range(6)] + [
            dma(2), dma(6, 6, 2), dma(6, 6, 2),
        ],
        compiler_params=pltpu.CompilerParams(
            collective_id=cid, has_side_effects=True, vmem_limit_bytes=56 << 20),
        cost_estimate=pl.CostEstimate(flops=2 * 1024 * 256 * 7168, bytes_accessed=1 << 23, transcendentals=0),
    )(act.reshape(cube + (8, 512)), down, others)


def slot(h):
    return (h % 2) * 16 + h // 2


def front_kernel(lengths, qn, qr, ka_hbm, ct_hbm, new, va_hbm, w0, w1, w2, w3, out, o0, o1, o2, o3, fresh, ka, ct, va, ropef, ropeb, wide,
                 qs, qg, rg, ats, atg, loads, q_s, q_r, r_s, r_r, a_s, a_r, x_s, x_r):
    x, y, z, c = place()
    e = (x * 4 + z) * 2 + c
    others = [(k - 1, (y + k) % 4) for k in range(1, 4)]
    fetch = [pltpu.make_async_copy(a, b, loads.at[n])
             for n, (a, b) in enumerate(((ka_hbm, ka), (ct_hbm, ct), (va_hbm, va)))]
    for copy in fetch:
        copy.start()
    barrier = pltpu.get_barrier_semaphore()
    for k, t in others:
        pl.semaphore_signal(barrier, inc=1, device_id=(e, t), device_id_type=MESH)
    sib = partner(x, y, z, c, SIBLING)
    pl.semaphore_signal(barrier, inc=1, device_id=sib, device_id_type=MESH)
    pl.semaphore_wait(barrier, 4)
    trade = [pltpu.make_async_remote_copy(
        src_ref=a, dst_ref=b, send_sem=x_s.at[n], recv_sem=x_r.at[n], device_id=sib, device_id_type=MESH)
        for n, (a, b) in enumerate(((w0, o0), (w1, o1), (w2, o2), (w3, o3)))]

    def rope_copy(k, t):
        return pltpu.make_async_remote_copy(
            src_ref=ropeb.at[t], dst_ref=rg.at[y], send_sem=r_s.at[k], recv_sem=r_r.at[k],
            device_id=(e, t), device_id_type=MESH)

    def query_copy(i, k, t):
        return pltpu.make_async_remote_copy(
            src_ref=qs.at[i, t], dst_ref=qg.at[i, y], send_sem=q_s.at[i, k], recv_sem=q_r.at[i, k],
            device_id=(e, t), device_id_type=MESH)

    def back_copy(i, k, t):
        return pltpu.make_async_remote_copy(
            src_ref=ats.at[i, t], dst_ref=atg.at[i, y], send_sem=a_s.at[i, k], recv_sem=a_r.at[i, k],
            device_id=(e, t), device_id_type=MESH)

    fresh[...] = new[...].astype(F32)
    for j in range(16):
        ropef[:, j, :] = qr[:, j * 128:(j + 1) * 128].astype(F32)
    ropeb[...] = ropef[...].astype(BF).reshape(4, 8, 16, 128)
    for k, t in others:
        rope_copy(k, t).start()
    rg[y] = ropeb[y]
    fetch[0].wait()
    for h in range(32):
        wide[:, slot(h), :] = jnp.dot(qn[:, h * 128:(h + 1) * 128], ka[h], preferred_element_type=F32)

    def push(i, carry):
        for k, t in others:
            qs[i, t] = wide[t * 8 + i].astype(BF)
            query_copy(i, k, t).start()
        qg[i, y] = wide[y * 8 + i].astype(BF)
        return carry

    lax.fori_loop(0, 8, push, 0)
    for copy in trade:
        copy.start()
    fetch[1].wait()
    for k, t in others:
        rope_copy(k, t).wait_recv()

    def attend(i, carry):
        for k, t in others:
            query_copy(i, k, t).wait_recv()
        q = qg[i].reshape(128, 512)
        ropes = [rg[t, i] for t in range(4)]
        ropes = jnp.concatenate([half for v in ropes for half in (v[:, :64], v[:, 64:])], axis=0)
        s = jnp.dot(q, ct[i, :512, :], preferred_element_type=F32)
        s = s + jnp.dot(ropes, ct[i, 512:, :], preferred_element_type=F32)
        scale = 1.0 / math.sqrt(192)
        inside = lax.broadcasted_iota(jnp.int32, (128, 512), 1) < lengths[i]
        s = jnp.where(inside, s * scale, -1e30)
        latest = fresh[pl.ds(i, 1), :]
        own = jnp.sum(q.astype(F32) * latest[:, :512], axis=1, keepdims=True)
        own = (own + jnp.sum(ropes.astype(F32) * latest[:, 512:], axis=1, keepdims=True)) * scale
        top = jnp.maximum(jnp.max(s, axis=1, keepdims=True), own)
        w = jnp.exp(s - top)
        own = jnp.exp(own - top)
        total = jnp.sum(w, axis=1, keepdims=True) + own
        a = lax.dot_general(w.astype(BF), ct[i, :512, :], (((1,), (1,)), ((), ())),
                            preferred_element_type=F32)
        a = (a + own * latest[:, :512]) / total
        ats[i] = a.astype(BF).reshape(4, 32, 512)
        for k, t in others:
            back_copy(i, k, t).start()
        atg[i, y] = ats[i, y]
        return carry

    lax.fori_loop(0, 8, attend, 0)

    def widen(i, carry):
        for k, t in others:
            back_copy(i, k, t).wait_recv()
        for t in range(4):
            wide[t * 8 + i] = atg[i, t].astype(F32)
        return carry

    lax.fori_loop(0, 8, widen, 0)
    fetch[2].wait()
    for h in range(32):
        v = wide[:, slot(h), :].astype(BF)
        out[:, h * 128:(h + 1) * 128] = jnp.dot(v, va[h], preferred_element_type=F32).astype(BF)

    def finish(i, carry):
        for k, t in others:
            query_copy(i, k, t).wait_send()
            back_copy(i, k, t).wait_send()
        return carry

    lax.fori_loop(0, 8, finish, 0)
    for k, t in others:
        rope_copy(k, t).wait_send()
    for copy in trade:
        copy.wait()


def front(lengths, qn, qr, ka, ct, new, va, weights, cid):
    inside = pl.BlockSpec(memory_space=pltpu.VMEM)
    outside = pl.BlockSpec(memory_space=pl.ANY)
    dma = lambda *shape: pltpu.SemaphoreType.DMA(shape)
    return pl.pallas_call(
        front_kernel,
        out_shape=(jax.ShapeDtypeStruct((32, 4096), BF),) + tuple(jax.ShapeDtypeStruct(w.shape, BF) for w in weights),
        in_specs=[pl.BlockSpec(memory_space=pltpu.SMEM), inside, inside, outside, outside, inside, outside]
        + [outside] * 4,
        out_specs=(inside,) + (outside,) * 4,
        scratch_shapes=[
            pltpu.VMEM((8, 576), F32),
            pltpu.VMEM((32, 128, 512), BF), pltpu.VMEM((8, 576, 512), BF), pltpu.VMEM((32, 512, 128), BF),
            pltpu.VMEM((32, 16, 128), F32), pltpu.VMEM((4, 8, 16, 128), BF), pltpu.VMEM((32, 32, 512), F32),
            pltpu.VMEM((8, 4, 32, 512), BF), pltpu.VMEM((8, 4, 32, 512), BF), pltpu.VMEM((4, 8, 16, 128), BF),
            pltpu.VMEM((8, 4, 32, 512), BF), pltpu.VMEM((8, 4, 32, 512), BF),
            dma(3), dma(8, 3), dma(8, 3), dma(3), dma(3), dma(8, 3), dma(8, 3), dma(4), dma(4),
        ],
        compiler_params=pltpu.CompilerParams(
            collective_id=cid, has_side_effects=True, vmem_limit_bytes=56 << 20),
        cost_estimate=pl.CostEstimate(flops=1 << 31, bytes_accessed=1 << 24, transcendentals=1 << 19),
    )(lengths, qn, qr, ka, ct, new, va, *weights)


def per_device(
    query_nope,
    query_rope,
    key_absorb,
    latent_cache,
    new_latent,
    context_lengths,
    value_absorb,
    out_proj,
    residual,
    norm_gain,
    routes,
    gate_weights,
    expert_gate,
    expert_up,
    expert_down,
):
    proj = jnp.swapaxes(out_proj, 0, 1)
    gate, up, down = expert_gate[0], expert_up[0], expert_down[0]
    head_out, proj2, gate2, up2, down2 = front(
        context_lengths, query_nope, query_rope, key_absorb, jnp.swapaxes(latent_cache, 1, 2),
        new_latent, value_absorb, (proj, gate, up, down), 0,
    )
    act, own = middle(
        head_out, proj, proj2, residual, norm_gain.reshape(32, 224), routes, gate_weights, (gate, up, gate2, up2), 1
    )
    routed = moe_out(act, down, down2, 2)
    hidden = own[:8].astype(F32) / norm_gain.astype(F32)[None, :]
    return (hidden + routed).astype(BF)


def solution(mesh):
    placed = (
        P("expert", "tensor"),
        P("expert", "tensor"),
        P("tensor", None, None),
        P(("expert", "tensor"), None, None),
        P(("expert", "tensor"), None),
        P(("expert", "tensor")),
        P("tensor", None, None),
        P("tensor", "expert"),
        P(("expert", "tensor"), None),
        P(),
        P(("expert", "tensor"), None),
        P(("expert", "tensor"), None),
        P("expert", None, "tensor"),
        P("expert", None, "tensor"),
        P("expert", "tensor", None),
    )
    return jax.shard_map(
        per_device,
        mesh=mesh,
        in_specs=placed,
        out_specs=P(("expert", "tensor"), None),
        check_vma=False,
    )
```

time: 930 us -> 163 us (0.18)
  waiting for transfers between devices: 777 us -> 0 us
  Pallas kernels: 0 us -> 160 us
  blocking collectives: 72.7 us -> 0 us
  matrix products: 35.7 us -> 0 us
  starting transfers between devices: 15.5 us -> 0 us
  between operations: 13.4 us -> 0.06 us
  local copies, waits for them, and re-layouts: 12 us -> 0.71 us
    reduce_scatter x2 -> x0, waiting for transfers between devices: 683 us -> none  [the longest x1 662 us: per_device(): lax.psum_scatter(partial_out.astype(jnp.bfloat16), ('expert', 'tensor'),...]
    pallas_call x0 -> x3, Pallas kernels: none -> 160 us  [the longest x1 88.2 us: middle(): pl.pallas_call(middle_kernel, out_shape=(jax.ShapeDtypeStruct((512, 512),...]
    all_gather x2 -> x0, waiting for transfers between devices: 70.5 us -> none  [the longest x1 53.5 us: per_device(): lax.all_gather(head_out, 'expert', axis=0, tiled=True)]
    all_gather x1 -> x0, blocking collectives: 56.7 us -> none  [per_device(): table = lax.all_gather(table, ('expert', 'tensor'), axis=0, tiled=True)]
    dot_general x9 -> x0, matrix products: 35.7 us -> none  [the longest x1 8.88 us: per_device(): jnp.dot(tokens, expert_gate[0], preferred_element_type=jnp.float32)]
    all_to_all x3 -> x0, waiting for transfers between devices: 23.1 us -> none  [the longest x1 13.8 us: per_device(): lax.all_to_all(absorbed, 'tensor', split_axis=0, concat_axis=1, tiled=True)]
    all_to_all x1 -> x0, blocking collectives: 16 us -> none  [per_device(): lax.all_to_all(attended, 'tensor', split_axis=1, concat_axis=0, tiled=True)]
    all_to_all x3 -> x0, starting transfers between devices: 15.3 us -> none  [the longest x1 7.23 us: per_device(): lax.all_to_all(summed, 'expert', split_axis=0, concat_axis=2, tiled=True)[0]]
  transfers between devices with their start and end apart: 7 -> 0, of which waited for: 7 -> 0; matrix products, arithmetic and copies ran while one was open for 1% -> 0% of each run, Pallas kernels for 0% -> 0%
where the time goes in v4:
time: 163 us
  Pallas kernels  160 us (98%)
  other arithmetic  1.64 us (1%)
    pallas_call x1, Pallas kernels, middle(): pl.pallas_call(middle_kernel, out_shape=(jax.ShapeDtypeStruct((512, 512),...  88.2 us
    pallas_call x1, Pallas kernels, moe_out(): pl.pallas_call(moe_out_kernel, out_shape=jax.ShapeDtypeStruct((8, 7168),...  37.4 us
    pallas_call x1, Pallas kernels, front(): pl.pallas_call(front_kernel, out_shape=(jax.ShapeDtypeStruct((32, 4096),...  34.8 us

profile of v4, /device:TPU:0, one launch (start us, length us, event | category | flops | bytes accessed | tf_op | source)
XLA Modules:
  0.0 162.8 jit_solution(13826901846284344081)
XLA Ops:
  0.0 0.0 copy-start
  0.0 34.8 %shard_map.145 = (bf16[32,4096]{1,0:T(8,128)(2,1)}, bf16[224,4096]{1,0:T(8,128)(2,1)}, bf16[7168,256]{1,0:T(8,128)(2,1)}, bf16[7168,256]{1,0:T(8,128)(2,1)}, bf16[256,7168]{1,0:T(8,128)(2,1)}) custom-call(s32[8]{0:T(128)} %lengths.1, bf16[32,4096]{1,0:T(8,128)(2,1)} %qn.1, bf16[32,2048]{1,0:T(8,128)(2,1)} %qr.1, bf16[32,128,512]{2,1,0:T(8,128)(2,1)} %ka_hbm.1, ...), custom_call_target="tpu_custom_call" | custom-call | flops 2147483648 | bytes 16777216 | tf_op jit(solution)/shard_map/pallas_call | solution.py:530
  34.8 0.0 copy-done
  34.8 0.7 reshape.13.gains
  35.5 88.2 %shard_map.146 = (f32[512,512]{1,0:T(8,128)}, bf16[16,7168]{1,0:T(8,128)(2,1)}) custom-call(bf16[32,4096]{1,0:T(8,128)(2,1)} %get-tuple-element.12.head, bf16[224,4096]{1,0:T(8,128)(2,1)} %bitcast.18, bf16[224,4096]{1,0:T(8,128)(2,1)} %get-tuple-element.13.proj2_hbm, bf16[8,7168]{1,0:T(8,128)(2,1)} %res.1, bf16[32,224]{1,0:T(8,128)(2,1)} %reshape.13.gains, ...), custom_call_target="tpu_custom_call" | custom-call | flops 7516192768 | bytes 8388608 | tf_op jit(solution)/shard_map/pallas_call | solution.py:279
  123.7 0.0 copy-start.1
  123.8 37.4 %shard_map.147 = f32[8,7168]{1,0:T(8,128)} custom-call(f32[2,2,2,2,2,2,8,512]{7,6,5,4,3,2,1,0:T(8,128)} %bitcast.21, bf16[256,7168]{1,0:T(8,128)(2,1)} %bitcast.16, bf16[256,7168]{1,0:T(8,128)(2,1)} %get-tuple-element.18.others_hbm), custom_call_target="tpu_custom_call" | custom-call | flops 3758096384 | bytes 8388608 | tf_op jit(solution)/shard_map/pallas_call | solution.py:391
  161.2 0.0 copy-done.1
  161.2 1.6 %add_convert_fusion = bf16[8,7168]{1,0:T(8,128)(2,1)} fusion(f32[8,7168]{1,0:T(8,128)} %shard_map.147, f32[7168]{0:T(1024)S(1)} %convert_element_type.10, bf16[16,7168]{1,0:T(8,128)(2,1)S(1)} %copy-done.1), kind=kLoop, calls=%fused_computation | loop fusion | flops 229376 | bytes 487424 | tf_op jit(solution)/shard_map/convert_element_type | solution.py:578
  (1 shorter events, 0.0 us)
Async XLA Ops:
  0.0 34.8 %copy-start = (bf16[7168]{0:T(1024)(128)(2,1)S(1)}, bf16[7168]{0:T(1024)(128)(2,1)}, u32[]{:S(2)}) copy-start(bf16[7168]{0:T(1024)(128)(2,1)} %param.24) | copy-start | bytes 43012
  123.7 37.4 %copy-start.1 = (bf16[16,7168]{1,0:T(8,128)(2,1)S(1)}, bf16[16,7168]{1,0:T(8,128)(2,1)}, u32[]{:S(2)}) copy-start(bf16[16,7168]{1,0:T(8,128)(2,1)} %get-tuple-element.16) | copy-start | bytes 688132

commit v5 on v4

v5 whole, which is shorter than its diff:
```python
import functools, math
import jax, jax.numpy as jnp
from jax import lax
from jax.experimental import pallas as pl
from jax.experimental.pallas import tpu as pltpu
from jax.sharding import PartitionSpec as P

MESH = pl.DeviceIdType.MESH
BF = jnp.bfloat16
F32 = jnp.float32
SIBLING = 6


def place():
    e, y = lax.axis_index("expert"), lax.axis_index("tensor")
    return e // 8, y, (e // 2) % 4, e % 2


def cube_bits(x, y, z):
    out = []
    for v in (y, x, z):
        g = jnp.where(v >= 2, 5 - v, v)
        out += [g // 2, g % 2]
    return out


def partner(x, y, z, c, d):
    if d == SIBLING:
        return ((x * 4 + z) * 2 + 1 - c, y)
    at = [y, x, z]
    v = at[d // 2]
    at[d // 2] = 3 - v if d % 2 == 0 else v + 1 - 2 * (v % 2)
    y, x, z = at
    return ((x * 4 + z) * 2 + c, y)


def meet(dims, x, y, z, c):
    barrier = pltpu.get_barrier_semaphore()
    for d in dims:
        pl.semaphore_signal(barrier, inc=1, device_id=partner(x, y, z, c, d), device_id_type=MESH)
    pl.semaphore_wait(barrier, len(dims))


FREE, OTHER, MINE = "free", "other", "mine"


def index_of(bits, spec):
    return [slice(None) if spec.get(d) == FREE else (1 - bits[d] if spec.get(d) == OTHER else bits[d])
            for d in range(6)]


class Gather:
    def __init__(self, order, cut, send_sem, recv_sem, where, split=True):
        self.order, self.cut, self.where, self.split = order, cut, where, split
        self.sems = send_sem, recv_sem
        self.copies = {}

    def send(self, s, part):
        o = self.order
        spec = {d: FREE for d in o[:max(s - 1, 0) if self.split else s]}
        if part:
            spec[o[s - 1]] = OTHER
        ref = self.cut(spec)
        copy = pltpu.make_async_remote_copy(
            src_ref=ref, dst_ref=ref, send_sem=self.sems[0].at[s, part], recv_sem=self.sems[1].at[s, part],
            device_id=partner(*self.where, o[s]), device_id_type=MESH)
        copy.start()
        self.copies[s, part] = copy

    def last(self, part):
        o = self.order
        spec = {d: FREE for d in o[:-2]}
        spec[o[-1]] = OTHER
        if part:
            spec[o[-2]] = OTHER
        return spec

    def turn(self, s):
        if s == 0:
            self.send(0, 0)
            if self.split:
                self.send(1, 0)
            return
        for part in (0, 1) if self.split and s > 1 else (0,):
            self.copies[s - 1, part].wait_recv()
        if s < len(self.order):
            if self.split:
                self.send(s, 1)
                if s + 1 < len(self.order):
                    self.send(s + 1, 0)
            else:
                self.send(s, 0)

    def finish(self, part):
        self.copies[len(self.order) - 1, part].wait_recv()

    def wait_sends(self):
        for copy in self.copies.values():
            copy.wait_send()


ROW_AT = (0, 80, 160, 240, 320, 384)
ROW_N = (80, 80, 80, 80, 64, 64)


def slot(h):
    return (h % 2) * 16 + h // 2


def main_kernel(lengths, qn, qr, ka_hbm, ct_hbm, new, va_hbm, proj_hbm, res, gains, routes, weights, gate_hbm, up_hbm,
                down_hbm, act, own, others,
                fresh, ka, ct, va, ropef, ropeb, wide, qs, qg, rg, ats, atg, proj, wts, heads, product, part, summed,
                gainf, turn, turnf, got, buf, sqb, acc, factors,
                loads, q_s, q_r, r_s, r_r, a_s, a_r, x_s, x_r, h_s, h_r, y_s, y_r, t_s, t_r, st_s, st_r):
    x, y, z, c = where = place()
    bits = cube_bits(x, y, z)
    yh, yl, xh, xl, zh, zl = bits
    chip = (x * 4 + z) * 2
    e = chip + c
    others_y = [(k - 1, (y + k) % 4) for k in range(1, 4)]
    sib = partner(x, y, z, c, SIBLING)
    fetch = [pltpu.make_async_copy(a, b, loads.at[n]) for n, (a, b) in enumerate((
        (ka_hbm, ka), (ct_hbm, ct), (va_hbm, va), (proj_hbm, proj.at[c]), (gate_hbm, wts.at[0, 0]),
        (up_hbm, wts.at[0, 1])))]
    for copy in fetch:
        copy.start()
    barrier = pltpu.get_barrier_semaphore()
    for d in range(7):
        pl.semaphore_signal(barrier, inc=1, device_id=partner(x, y, z, c, d), device_id_type=MESH)
    pl.semaphore_signal(barrier, inc=1, device_id=(e, (y + 2) % 4), device_id_type=MESH)
    fresh[...] = new[...].astype(F32)
    for j in range(16):
        ropef[:, j, :] = qr[:, j * 128:(j + 1) * 128].astype(F32)
    ropeb[...] = ropef[...].astype(BF).reshape(4, 8, 16, 128)
    pl.semaphore_wait(barrier, 8)
    trade = [pltpu.make_async_remote_copy(
        src_ref=a, dst_ref=b, send_sem=x_s.at[n], recv_sem=x_r.at[n], device_id=sib, device_id_type=MESH)
        for n, (a, b) in enumerate((
            (proj_hbm, proj.at[c]), (gate_hbm, wts.at[1, 0]), (up_hbm, wts.at[1, 1]), (down_hbm, others)))]

    def rope_copy(k, t):
        return pltpu.make_async_remote_copy(
            src_ref=ropeb.at[t], dst_ref=rg.at[y], send_sem=r_s.at[k], recv_sem=r_r.at[k],
            device_id=(e, t), device_id_type=MESH)

    def query_copy(i, k, t):
        return pltpu.make_async_remote_copy(
            src_ref=qs.at[i, t], dst_ref=qg.at[i, y], send_sem=q_s.at[i, k], recv_sem=q_r.at[i, k],
            device_id=(e, t), device_id_type=MESH)

    def back_copy(i, k, t):
        return pltpu.make_async_remote_copy(
            src_ref=ats.at[i, t], dst_ref=atg.at[i, y], send_sem=a_s.at[i, k], recv_sem=a_r.at[i, k],
            device_id=(e, t), device_id_type=MESH)

    fresh[...] = new[...].astype(F32)
    for k, t in others_y:
        rope_copy(k, t).start()
    rg[y] = ropeb[y]
    fetch[0].wait()
    for h in range(32):
        wide[:, slot(h), :] = jnp.dot(qn[:, h * 128:(h + 1) * 128], ka[h], preferred_element_type=F32)

    def push(i, carry):
        for k, t in others_y:
            qs[i, t] = wide[t * 8 + i].astype(BF)
            query_copy(i, k, t).start()
        qg[i, y] = wide[y * 8 + i].astype(BF)
        return carry

    lax.fori_loop(0, 4, push, 0)
    for copy in trade:
        copy.start()

    turn[...] = jnp.zeros_like(turn)
    part[...] = jnp.zeros_like(part)
    for k in range(16):
        sx, sz = k // 4 ^ k // 8, k % 4 ^ k % 4 // 2
        v = [res[:, n * 224:(n + 1) * 224].astype(F32) for n in (2 * k, 2 * k + 1)]
        turn[sx // 2, sx % 2, sz // 2, sz % 2, :, :224] = jnp.concatenate(v, axis=0).astype(BF)
    for k in range(32):
        gainf[k:k + 1, :] = gains[:, k * 224:(k + 1) * 224].astype(F32)
    lane = lax.broadcasted_iota(jnp.int32, (8, 128), 1)
    table = jnp.zeros((8, 128), F32)
    for k in range(8):
        table = table + jnp.where(lane == routes[:, k:k + 1], weights[:, k:k + 1], 0.0)
    acc[...] = jnp.zeros_like(acc)
    fetch[1].wait()
    for k, t in others_y:
        rope_copy(k, t).wait_recv()

    def attend(i, carry):
        for k, t in others_y:
            query_copy(i, k, t).wait_recv()
        q = qg[i].reshape(128, 512)
        ropes = [rg[t, i] for t in range(4)]
        ropes = jnp.concatenate([half for v in ropes for half in (v[:, :64], v[:, 64:])], axis=0)
        s = jnp.dot(q, ct[i, :512, :], preferred_element_type=F32)
        s = s + jnp.dot(ropes, ct[i, 512:, :], preferred_element_type=F32)
        scale = 1.0 / math.sqrt(192)
        inside = lax.broadcasted_iota(jnp.int32, (128, 512), 1) < lengths[i]
        s = jnp.where(inside, s * scale, -1e30)
        latest = fresh[pl.ds(i, 1), :]
        own = jnp.sum(q.astype(F32) * latest[:, :512], axis=1, keepdims=True)
        own = (own + jnp.sum(ropes.astype(F32) * latest[:, 512:], axis=1, keepdims=True)) * scale
        top = jnp.maximum(jnp.max(s, axis=1, keepdims=True), own)
        w = jnp.exp(s - top)
        own = jnp.exp(own - top)
        total = jnp.sum(w, axis=1, keepdims=True) + own
        a = lax.dot_general(w.astype(BF), ct[i, :512, :], (((1,), (1,)), ((), ())),
                            preferred_element_type=F32)
        a = (a + own * latest[:, :512]) / total
        ats[i] = a.astype(BF).reshape(4, 32, 512)
        for k, t in others_y:
            back_copy(i, k, t).start()
        atg[i, y] = ats[i, y]
        return carry

    lax.fori_loop(0, 4, attend, 0)
    lax.fori_loop(4, 8, push, 0)

    def head_cut(n, p):
        def cut(spec):
            g = index_of(bits, spec)
            return heads.at[n, g[2], g[3], g[4], g[5], :, pl.ds(p * 1024, 1024)]
        return cut

    first = [[Gather([2 + (p + i) % 4 for i in range(4)], head_cut(n, p), h_s.at[n, p], h_r.at[n, p], where)
              for p in range(4)] for n in range(2)]

    def head_out(n):
        def widen(i, carry):
            for k, t in others_y:
                back_copy(n * 4 + i, k, t).wait_recv()
            for t in range(4):
                wide[n * 16 + t * 4 + i] = atg[n * 4 + i, t].astype(F32)
            return carry

        lax.fori_loop(0, 4, widen, 0)
        for h in range(32):
            v = wide[n * 16:n * 16 + 16, slot(h), :].astype(BF)
            o = jnp.dot(v, va[h], preferred_element_type=F32)
            heads[n, xh, xl, zh, zl, :, h * 128:(h + 1) * 128] = o.astype(BF)

    def residual_turn(k):
        d = 2 + k
        at = tuple(1 - bits[d] if m == d else slice(None) for m in (2, 3, 4, 5))
        copy = pltpu.make_async_remote_copy(
            src_ref=turn.at[at], dst_ref=got.at[k], send_sem=t_s.at[k], recv_sem=t_r.at[k],
            device_id=partner(x, y, z, c, d), device_id_type=MESH)
        copy.start()
        return copy, at

    def project(n):
        v = heads[n].reshape(256, 4096)
        for m in range(2):
            o = lax.dot_general(v, proj[m], (((1,), (1,)), ((), ())), preferred_element_type=F32)
            product[...] = o.reshape(16, 16, 224)
            for t in range(4):
                rows = [product[:, t * 4 + i, :] for i in range(4)]
                part[n, t, m, :, :224] = jnp.concatenate(rows, axis=0).astype(BF)
        copies = []
        for k, t in others_y:
            copy = pltpu.make_async_remote_copy(
                src_ref=part.at[n, t], dst_ref=summed.at[n, k], send_sem=y_s.at[n, k], recv_sem=y_r.at[n, k],
                device_id=(e, t), device_id_type=MESH)
            copy.start()
            copies.append(copy)
        return copies

    fetch[2].wait()
    head_out(0)
    turning = None
    for s in range(4):
        for g in first[0]:
            g.turn(s)
        if turning is not None:
            turning[0].wait()
            turn[turning[1]] = got[s - 1]
        turning = residual_turn(s)
        attend(4 + s, 0)
    head_out(1)
    for s in range(2):
        for g in first[1]:
            g.turn(s)
    for half in range(2):
        for g in first[0]:
            g.finish(half)
    for g in first[1]:
        g.turn(2)
    fetch[3].wait()
    trade[0].wait_recv()
    copies = [project(0)]
    for g in first[1]:
        g.turn(3)
    turning[0].wait()
    turn[turning[1]] = got[3]
    turnf[...] = turn[...].astype(F32).reshape(16, 16, 256)
    for half in range(2):
        for g in first[1]:
            g.finish(half)
    copies.append(project(1))
    sums = []
    for n in range(2):
        total = part[n, y].astype(F32)
        for k, copy in enumerate(copies[n]):
            copy.wait_recv()
            total = total + summed[n, k].astype(F32)
        sums.append(total[:, :, :224].astype(BF).astype(F32))
    squares, hid = 0.0, []
    for m in range(2):
        hidden = jnp.concatenate([sums[0][m], sums[1][m]], axis=0)
        hidden = hidden + jnp.concatenate([turnf[:, m * 8 + i, :224] for i in range(8)], axis=0)
        squares = squares + jnp.sum(hidden * hidden, axis=1, keepdims=True)
        hid.append((hidden * gainf[pl.ds(chip + m, 1), :]).T)
    lane3 = lax.broadcasted_iota(jnp.int32, (8, 16, 128), 2)
    from3 = lax.broadcasted_iota(jnp.int32, (8, 16, 128), 1)
    spread = jnp.sum(jnp.where(lane3 == from3 + 32, squares.reshape(8, 16, 1), 0.0), axis=1)
    sqb[yh, yl, xh, xl, zh, zl] = table + spread
    buf[xh, xl, yh, yl, zh, zl] = jnp.concatenate(hid, axis=0).astype(BF)

    def cut_of(p):
        def cut(spec):
            g = index_of(bits, spec)
            if p == 6:
                return sqb.at[g[0], g[1], g[2], g[3], g[4], g[5]]
            return buf.at[g[2], g[3], g[0], g[1], g[4], g[5], pl.ds(ROW_AT[p], ROW_N[p]), :]
        return cut

    def order_of(p):
        return [((4 if p == 6 else p) + k) % 6 for k in range(6)]

    second = [Gather(order_of(p), cut_of(p), st_s.at[p], st_r.at[p], where, p < 6) for p in range(7)]

    def work(p, spec):
        rows = pl.ds(ROW_AT[p], ROW_N[p])
        opts = [(0, 1) if spec.get(d) == FREE else ((1 - bits[d],) if spec.get(d) == OTHER else (bits[d],))
                for d in range(6)]
        inner = [(i, j, k, l) for i in opts[2] for j in opts[3] for k in opts[4] for l in opts[5]]
        outer = [(a, b) for a in opts[0] for b in opts[1]]
        lhs = []
        for a, b in outer:
            slab = [buf[i, j, a, b, k, l, rows, :] for i, j, k, l in inner]
            lhs.append(jnp.concatenate(slab, axis=0).T)
        lhs = jnp.concatenate(lhs, axis=0)
        for n in range(2):
            for m in range(2):
                v = [wts[n, m, 2 * i + (i + j - 2 * i * j), 2 * k + (k + l - 2 * k * l), rows, :]
                     for i, j, k, l in inner]
                o = jnp.dot(lhs, jnp.concatenate(v, axis=0), preferred_element_type=F32)
                for q, (a, b) in enumerate(outer):
                    acc[n, m, a, b] += o[q * 128:(q + 1) * 128]

    for s in range(6):
        for g in second:
            g.turn(s)
    for copy in fetch[4:]:
        copy.wait()
    for copy in trade[1:3]:
        copy.wait_recv()
    for p in range(6):
        work(p, {d: FREE for d in order_of(p)[:5]})
    second[6].turn(6)
    lane = lax.broadcasted_iota(jnp.int32, (128, 128), 1)
    block = lax.broadcasted_iota(jnp.int32, (128, 128), 0) % 16
    for t in range(4):
        info = jnp.concatenate([sqb[t // 2, t % 2, :, :, :, :, i, :].reshape(16, 128) for i in range(8)], axis=0)
        total = jnp.sum(info.reshape(8, 16, 128), axis=1, keepdims=True)
        total = jnp.broadcast_to(total, (8, 16, 128)).reshape(128, 128)
        total = jnp.sum(jnp.where(lane == block + 32, total, 0.0), axis=1, keepdims=True)
        scale = lax.rsqrt(total / 7168.0 + 1e-6)
        for n in range(2):
            expert = chip + (c if n == 0 else 1 - c)
            wt = jnp.sum(jnp.where(lane == expert, info, 0.0), axis=1, keepdims=True)
            factors[t, n] = jnp.where(lane == 0, scale, wt)
    for half in range(2):
        for p in range(6):
            second[p].finish(half)
            work(p, second[p].last(half))
    for t in range(4):
        for n in range(2):
            scale, wt = factors[t, n, :, 0:1], factors[t, n, :, 1:2]
            g = acc[n, 0, t // 2, t % 2] * scale
            u = acc[n, 1, t // 2, t % 2] * scale
            a = g * u / (1.0 + jnp.exp(-g)) * wt
            for i in range(8):
                act[t * 16:(t + 1) * 16, i, n * 256:(n + 1) * 256] = a[i * 16:(i + 1) * 16]
    spot = (xh * 2 + xl) * 4 + zh * 2 + zl
    row = lax.broadcasted_iota(jnp.int32, (16, 128), 0)
    pick = (lax.broadcasted_iota(jnp.int32, (16, 128), 1) == row * 16 + spot) & (row < 8)
    pick = jnp.where(pick, 1.0, 0.0).astype(BF)
    for j in range(4):
        v = jnp.concatenate([buf[j // 2, j % 2, yh, yl, k // 2, k % 2] for k in (0, 1, 3, 2)], axis=0)
        v = lax.dot_general(pick, v, (((1,), (1,)), ((), ())), preferred_element_type=F32)
        ax = j if j < 2 else 5 - j
        own[:, ax * 1792:(ax + 1) * 1792] = v.astype(BF)

    def finish(i, carry):
        for k, t in others_y:
            query_copy(i, k, t).wait_send()
            back_copy(i, k, t).wait_send()
        return carry

    lax.fori_loop(0, 8, finish, 0)
    for k, t in others_y:
        rope_copy(k, t).wait_send()
    for copy in trade:
        copy.wait_send()
    trade[3].wait_recv()
    for g in first[0] + first[1] + second:
        g.wait_sends()
    for copy in copies[0] + copies[1]:
        copy.wait_send()


def main(lengths, qn, qr, ka, ct, new, va, proj, res, gains, routes, weights, gate, up, down, cid):
    vm = lambda shape, kind=BF: pltpu.VMEM(shape, kind)
    dma = lambda *shape: pltpu.SemaphoreType.DMA(shape)
    two = lambda n: (2,) * n
    inside = pl.BlockSpec(memory_space=pltpu.VMEM)
    outside = pl.BlockSpec(memory_space=pl.ANY)
    return pl.pallas_call(
        main_kernel,
        out_shape=(jax.ShapeDtypeStruct((64, 8, 512), F32), jax.ShapeDtypeStruct((16, 7168), BF),
                   jax.ShapeDtypeStruct(down.shape, BF)),
        in_specs=[pl.BlockSpec(memory_space=pltpu.SMEM), inside, inside, outside, outside, inside, outside, outside]
        + [inside] * 4 + [outside] * 3,
        out_specs=(inside, inside, outside),
        scratch_shapes=[
            vm((8, 576), F32), vm((32, 128, 512)), vm((8, 576, 512)), vm((32, 512, 128)),
            vm((32, 16, 128), F32), vm((4, 8, 16, 128)), vm((32, 32, 512), F32),
            vm((8, 4, 32, 512)), vm((8, 4, 32, 512)), vm((4, 8, 16, 128)),
            vm((8, 4, 32, 512)), vm((8, 4, 32, 512)),
            vm((2, 224, 4096)), vm((2, 2, 4, 4, 448, 256)),
            vm((2,) + two(4) + (16, 4096)), vm((16, 16, 224), F32),
            vm((2, 4, 2, 64, 256)), vm((2, 3, 2, 64, 256)),
            vm((32, 224), F32), vm(two(4) + (16, 256)), vm((16, 16, 256), F32), vm((4,) + two(3) + (16, 256)),
            vm(two(6) + (448, 128)), vm(two(6) + (8, 128), F32), vm((2, 2, 2, 2, 128, 256), F32), vm((4, 2, 128, 128), F32),
            dma(6), dma(8, 3), dma(8, 3), dma(3), dma(3), dma(8, 3), dma(8, 3), dma(4), dma(4),
            dma(2, 4, 4, 2), dma(2, 4, 4, 2), dma(2, 3), dma(2, 3), dma(4), dma(4), dma(7, 6, 2), dma(7, 6, 2),
        ],
        compiler_params=pltpu.CompilerParams(
            collective_id=cid, has_side_effects=True, vmem_limit_bytes=62 << 20),
        cost_estimate=pl.CostEstimate(
            flops=1 << 34, bytes_accessed=1 << 25, transcendentals=1 << 20),
    )(lengths, qn, qr, ka, ct, new, va, proj, res, gains, routes, weights,
      gate.reshape(4, 4, 448, 256), up.reshape(4, 4, 448, 256), down)


OUT_W = (640, 640, 640, 640, 512, 512)
OUT_AT = (0, 640, 1280, 1920, 2560, 3072)


def moe_out_kernel(act, down_hbm, others_hbm, out, down, ps, r0, r1, r2, r3, r4, r5, loads, st_s, st_r):
    x, y, z, c = place()
    bits = cube_bits(x, y, z)
    rs = (r0, r1, r2, r3, r4, r5)
    fetch = []
    for p in range(6):
        for n, at in enumerate((OUT_AT[p], 3584 + OUT_AT[p])):
            for m, ref in enumerate((down_hbm, others_hbm)):
                copy = pltpu.make_async_copy(
                    ref.at[:, pl.ds(at, OUT_W[p])], down.at[pl.ds(m * 256, 256), pl.ds(at, OUT_W[p])],
                    loads.at[p, n * 2 + m])
                copy.start()
                fetch.append(copy)
    meet(range(6), x, y, z, c)

    def cut(ref, p, spec):
        idx = tuple(bits[d] if spec[d] == MINE else (1 - bits[d] if spec[d] == OTHER else slice(None))
                    for d in range(6) if d in spec)
        return ref.at[idx + (slice(None), pl.ds(OUT_AT[p], OUT_W[p]))]

    def spec_of(p, s, which):
        spec = {d: FREE for d in range(6)}
        for k in range(s):
            spec[(p + k) % 6] = MINE
        spec[(p + s) % 6] = OTHER
        if s < 5:
            spec[(p + s + 1) % 6] = OTHER if which == 0 else MINE
        return spec

    def product(p, spec):
        rows = act[tuple(bits[d] if spec[d] == MINE else (1 - bits[d] if spec[d] == OTHER else slice(None))
                         for d in range(6))]
        free = sum(spec[d] == FREE for d in range(6))
        rows = rows.reshape(8 << free, 512).astype(BF)
        halves = []
        for at in (OUT_AT[p], 3584 + OUT_AT[p]):
            o = jnp.dot(rows, down[:, at:at + OUT_W[p]], preferred_element_type=F32)
            halves.append(o.reshape(1 << free, 8, OUT_W[p]))
        got = jnp.concatenate(halves, axis=1).astype(BF)
        cut(ps, p, spec)[...] = got.reshape((2,) * free + (16, OUT_W[p]))

    sends = {}

    def landing(p, s, which):
        spec = spec_of(p, s, which)
        return cut(rs[s], p, {d: spec[d] for d in range(6) if d not in [(p + k) % 6 for k in range(s + 1)]})

    def send(p, s, which):
        copy = pltpu.make_async_remote_copy(
            src_ref=cut(ps, p, spec_of(p, s, which)), dst_ref=landing(p, s, which),
            send_sem=st_s.at[s, p, which], recv_sem=st_r.at[s, p, which],
            device_id=partner(x, y, z, c, (p + s) % 6), device_id_type=MESH)
        copy.start()
        sends[p, s, which] = copy

    def take(p, s, which):
        sends[p, s, which].wait_recv()
        spec = dict(spec_of(p, s, which))
        spec[(p + s) % 6] = MINE
        here, other = cut(ps, p, spec), landing(p, s, which)
        here[...] = (here[...].astype(F32) + other[...].astype(F32)).astype(BF)

    for which in (0, 1):
        for p in range(6):
            if which == 0:
                for copy in fetch[p * 4:p * 4 + 4]:
                    copy.wait()
            product(p, spec_of(p, 0, which))
            send(p, 0, which)
    for p in range(6):
        product(p, {d: MINE if d == p else FREE for d in range(6)})
    for s in range(5):
        for p in range(6):
            take(p, s, 0)
            send(p, s + 1, 0)
            if s < 4:
                send(p, s + 1, 1)
        for p in range(6):
            take(p, s, 1)
    for p in range(6):
        take(p, 5, 0)
    mine = ps[tuple(bits)].astype(F32)
    out[:, :3584] = mine[:8]
    out[:, 3584:] = mine[8:]
    for copy in sends.values():
        copy.wait_send()


def moe_out(act, down, others, cid):
    cube = (2,) * 6
    dma = lambda *shape: pltpu.SemaphoreType.DMA(shape)
    inside = pl.BlockSpec(memory_space=pltpu.VMEM)
    outside = pl.BlockSpec(memory_space=pl.ANY)
    return pl.pallas_call(
        moe_out_kernel,
        out_shape=jax.ShapeDtypeStruct((8, 7168), F32),
        in_specs=[inside, outside, outside],
        out_specs=inside,
        scratch_shapes=[
            pltpu.VMEM((512, 7168), BF),
            pltpu.VMEM(cube + (16, 3584), BF),
        ] + [pltpu.VMEM((2,) * (5 - s) + (16, 3584), BF) for s in range(6)] + [
            dma(6, 4), dma(6, 6, 2), dma(6, 6, 2),
        ],
        compiler_params=pltpu.CompilerParams(
            collective_id=cid, has_side_effects=True, vmem_limit_bytes=56 << 20),
        cost_estimate=pl.CostEstimate(flops=2 * 1024 * 256 * 7168, bytes_accessed=1 << 23, transcendentals=0),
    )(act.reshape(cube + (8, 512)), down, others)


def per_device(
    query_nope,
    query_rope,
    key_absorb,
    latent_cache,
    new_latent,
    context_lengths,
    value_absorb,
    out_proj,
    residual,
    norm_gain,
    routes,
    gate_weights,
    expert_gate,
    expert_up,
    expert_down,
):
    act, own, others = main(
        context_lengths, query_nope, query_rope, key_absorb, jnp.swapaxes(latent_cache, 1, 2), new_latent,
        value_absorb, jnp.swapaxes(out_proj, 0, 1), residual, norm_gain[None, :], routes, gate_weights,
        expert_gate[0], expert_up[0], expert_down[0], 1,
    )
    routed = moe_out(act, expert_down[0], others, 2)
    hidden = own[:8].astype(F32) / norm_gain.astype(F32)[None, :]
    return (hidden + routed).astype(BF)


def solution(mesh):
    placed = (
        P("expert", "tensor"),
        P("expert", "tensor"),
        P("tensor", None, None),
        P(("expert", "tensor"), None, None),
        P(("expert", "tensor"), None),
        P(("expert", "tensor")),
        P("tensor", None, None),
        P("tensor", "expert"),
        P(("expert", "tensor"), None),
        P(),
        P(("expert", "tensor"), None),
        P(("expert", "tensor"), None),
        P("expert", None, "tensor"),
        P("expert", None, "tensor"),
        P("expert", "tensor", None),
    )
    return jax.shard_map(
        per_device,
        mesh=mesh,
        in_specs=placed,
        out_specs=P(("expert", "tensor"), None),
        check_vma=False,
    )
```

time: 163 us -> 157 us (0.963)
  Pallas kernels: 160 us -> 154 us
    pallas_call x2 -> x1, Pallas kernels: 123 us -> 119 us  [main(): pl.pallas_call(main_kernel, out_shape=(jax.ShapeDtypeStruct((64, 8, 512),...]
    pallas_call x1, Pallas kernels: 37.4 us -> 34.9 us  [moe_out(): pl.pallas_call(moe_out_kernel, out_shape=jax.ShapeDtypeStruct((8, 7168),...]
where the time goes in v5:
time: 157 us
  Pallas kernels  154 us (98%)
  other arithmetic  1.64 us (1%)
    pallas_call x1, Pallas kernels, main(): pl.pallas_call(main_kernel, out_shape=(jax.ShapeDtypeStruct((64, 8, 512),...  119 us
    pallas_call x1, Pallas kernels, moe_out(): pl.pallas_call(moe_out_kernel, out_shape=jax.ShapeDtypeStruct((8, 7168),...  34.9 us

profile of v5, /device:TPU:0, one launch (start us, length us, event | category | flops | bytes accessed | tf_op | source)
XLA Modules:
  0.0 156.7 jit_solution(17774536345242227449)
XLA Ops:
  0.0 1.3 broadcast_in_dim.4.gains
  1.3 118.8 %shard_map.145 = (f32[64,8,512]{2,1,0:T(8,128)}, bf16[16,7168]{1,0:T(8,128)(2,1)}, bf16[256,7168]{1,0:T(8,128)(2,1)}) custom-call(s32[8]{0:T(128)} %lengths.1, bf16[32,4096]{1,0:T(8,128)(2,1)} %qn.1, bf16[32,2048]{1,0:T(8,128)(2,1)} %qr.1, bf16[32,128,512]{2,1,0:T(8,128)(2,1)} %ka_hbm.1, bf16[8,576,512]{2,1,0:T(8,128)(2,1)} %bitcast.6, bf16[8,576]{1,0:T(8,128)(2,1)} %new.1, ...), custom_call_target="tpu_custom_call" | custom-call | flops 17179869184 | bytes 33554432 | tf_op jit(solution)/shard_map/pallas_call | solution.py:422
  120.1 0.0 copy-start.1
  120.1 0.0 copy-start
  120.2 34.9 %shard_map.146 = f32[8,7168]{1,0:T(8,128)} custom-call(f32[2,2,2,2,2,2,8,512]{7,6,5,4,3,2,1,0:T(8,128)} %bitcast.12, bf16[256,7168]{1,0:T(8,128)(2,1)} %bitcast.10, bf16[256,7168]{1,0:T(8,128)(2,1)} %get-tuple-element.10.others_hbm), custom_call_target="tpu_custom_call" | custom-call | flops 3758096384 | bytes 8388608 | tf_op jit(solution)/shard_map/pallas_call | solution.py:547
  155.0 0.0 copy-done.1
  155.1 0.0 copy-done
  155.1 1.6 %add_convert_fusion = bf16[8,7168]{1,0:T(8,128)(2,1)} fusion(f32[8,7168]{1,0:T(8,128)} %shard_map.146, f32[7168]{0:T(1024)S(1)} %convert_element_type.10, bf16[16,7168]{1,0:T(8,128)(2,1)S(1)} %copy-done), kind=kLoop, calls=%fused_computation | loop fusion | flops 229376 | bytes 487424 | tf_op jit(solution)/shard_map/convert_element_type | solution.py:588
  (1 shorter events, 0.0 us)
Async XLA Ops:
  120.1 34.9 %copy-start.1 = (bf16[7168]{0:T(1024)(128)(2,1)S(1)}, bf16[7168]{0:T(1024)(128)(2,1)}, u32[]{:S(2)}) copy-start(bf16[7168]{0:T(1024)(128)(2,1)} %param.24) | copy-start | bytes 43012
  120.1 34.9 %copy-start = (bf16[16,7168]{1,0:T(8,128)(2,1)S(1)}, bf16[16,7168]{1,0:T(8,128)(2,1)}, u32[]{:S(2)}) copy-start(bf16[16,7168]{1,0:T(8,128)(2,1)} %get-tuple-element.8) | copy-start | bytes 688132

commit v6 on v5

--- a/solution.py
+++ b/solution.py
@@ -216,32 +216,6 @@
         atg[i, y] = ats[i, y]
         return carry
 
-    lax.fori_loop(0, 4, attend, 0)
-    lax.fori_loop(4, 8, push, 0)
-
-    def head_cut(n, p):
-        def cut(spec):
-            g = index_of(bits, spec)
-            return heads.at[n, g[2], g[3], g[4], g[5], :, pl.ds(p * 1024, 1024)]
-        return cut
-
-    first = [[Gather([2 + (p + i) % 4 for i in range(4)], head_cut(n, p), h_s.at[n, p], h_r.at[n, p], where)
-              for p in range(4)] for n in range(2)]
-
-    def head_out(n):
-        def widen(i, carry):
-            for k, t in others_y:
-                back_copy(n * 4 + i, k, t).wait_recv()
-            for t in range(4):
-                wide[n * 16 + t * 4 + i] = atg[n * 4 + i, t].astype(F32)
-            return carry
-
-        lax.fori_loop(0, 4, widen, 0)
-        for h in range(32):
-            v = wide[n * 16:n * 16 + 16, slot(h), :].astype(BF)
-            o = jnp.dot(v, va[h], preferred_element_type=F32)
-            heads[n, xh, xl, zh, zl, :, h * 128:(h + 1) * 128] = o.astype(BF)
-
     def residual_turn(k):
         d = 2 + k
         at = tuple(1 - bits[d] if m == d else slice(None) for m in (2, 3, 4, 5))
@@ -250,6 +224,36 @@
             device_id=partner(x, y, z, c, d), device_id_type=MESH)
         copy.start()
         return copy, at
+
+    turning = residual_turn(0)
+    lax.fori_loop(0, 4, attend, 0)
+    turning[0].wait()
+    turn[turning[1]] = got[0]
+    turning = residual_turn(1)
+    lax.fori_loop(4, 8, push, 0)
+
+    def head_cut(n, p):
+        def cut(spec):
+            g = index_of(bits, spec)
+            return heads.at[n, g[2], g[3], g[4], g[5], :, pl.ds(p * 1024, 1024)]
+        return cut
+
+    first = [[Gather([2 + (p + i) % 4 for i in range(4)], head_cut(n, p), h_s.at[n, p], h_r.at[n, p], where)
+              for p in range(4)] for n in range(2)]
+
+    def head_out(n):
+        def widen(i, carry):
+            for k, t in others_y:
+                back_copy(n * 4 + i, k, t).wait_recv()
+            for t in range(4):
+                wide[n * 16 + t * 4 + i] = atg[n * 4 + i, t].astype(F32)
+            return carry
+
+        lax.fori_loop(0, 4, widen, 0)
+        for h in range(32):
+            v = wide[n * 16:n * 16 + 16, slot(h), :].astype(BF)
+            o = jnp.dot(v, va[h], preferred_element_type=F32)
+            heads[n, xh, xl, zh, zl, :, h * 128:(h + 1) * 128] = o.astype(BF)
 
     def project(n):
         v = heads[n].reshape(256, 4096)
@@ -270,14 +274,13 @@
 
     fetch[2].wait()
     head_out(0)
-    turning = None
     for s in range(4):
         for g in first[0]:
             g.turn(s)
-        if turning is not None:
+        if s < 2:
             turning[0].wait()
-            turn[turning[1]] = got[s - 1]
-        turning = residual_turn(s)
+            turn[turning[1]] = got[s + 1]
+            turning = residual_turn(2 + s)
         attend(4 + s, 0)
     head_out(1)
     for s in range(2):

time: 157 us -> 155 us (0.987)
  Pallas kernels: 154 us -> 152 us
    pallas_call x1, Pallas kernels: 119 us -> 117 us  [main(): pl.pallas_call(main_kernel, out_shape=(jax.ShapeDtypeStruct((64, 8, 512),...]
where the time goes in v6:
time: 155 us
  Pallas kernels  152 us (98%)
  other arithmetic  1.64 us (1%)
    pallas_call x1, Pallas kernels, main(): pl.pallas_call(main_kernel, out_shape=(jax.ShapeDtypeStruct((64, 8, 512),...  117 us
    pallas_call x1, Pallas kernels, moe_out(): pl.pallas_call(moe_out_kernel, out_shape=jax.ShapeDtypeStruct((8, 7168),...  34.6 us

profile of v6, /device:TPU:0, one launch (start us, length us, event | category | flops | bytes accessed | tf_op | source)
XLA Modules:
  0.0 154.6 jit_solution(3593998013318082828)
XLA Ops:
  0.0 1.3 broadcast_in_dim.4.gains
  1.3 117.0 %shard_map.145 = (f32[64,8,512]{2,1,0:T(8,128)}, bf16[16,7168]{1,0:T(8,128)(2,1)}, bf16[256,7168]{1,0:T(8,128)(2,1)}) custom-call(s32[8]{0:T(128)} %lengths.1, bf16[32,4096]{1,0:T(8,128)(2,1)} %qn.1, bf16[32,2048]{1,0:T(8,128)(2,1)} %qr.1, bf16[32,128,512]{2,1,0:T(8,128)(2,1)} %ka_hbm.1, bf16[8,576,512]{2,1,0:T(8,128)(2,1)} %bitcast.6, bf16[8,576]{1,0:T(8,128)(2,1)} %new.1, ...), custom_call_target="tpu_custom_call" | custom-call | flops 17179869184 | bytes 33554432 | tf_op jit(solution)/shard_map/pallas_call | solution.py:425
  118.4 0.0 copy-start.1
  118.4 0.0 copy-start
  118.4 34.6 %shard_map.146 = f32[8,7168]{1,0:T(8,128)} custom-call(f32[2,2,2,2,2,2,8,512]{7,6,5,4,3,2,1,0:T(8,128)} %bitcast.12, bf16[256,7168]{1,0:T(8,128)(2,1)} %bitcast.10, bf16[256,7168]{1,0:T(8,128)(2,1)} %get-tuple-element.10.others_hbm), custom_call_target="tpu_custom_call" | custom-call | flops 3758096384 | bytes 8388608 | tf_op jit(solution)/shard_map/pallas_call | solution.py:550
  153.0 0.0 copy-done.1
  153.0 0.0 copy-done
  153.0 1.6 %add_convert_fusion = bf16[8,7168]{1,0:T(8,128)(2,1)} fusion(f32[8,7168]{1,0:T(8,128)} %shard_map.146, f32[7168]{0:T(1024)S(1)} %convert_element_type.10, bf16[16,7168]{1,0:T(8,128)(2,1)S(1)} %copy-done), kind=kLoop, calls=%fused_computation | loop fusion | flops 229376 | bytes 487424 | tf_op jit(solution)/shard_map/convert_element_type | solution.py:591
  (1 shorter events, 0.0 us)
Async XLA Ops:
  118.4 34.6 %copy-start.1 = (bf16[7168]{0:T(1024)(128)(2,1)S(1)}, bf16[7168]{0:T(1024)(128)(2,1)}, u32[]{:S(2)}) copy-start(bf16[7168]{0:T(1024)(128)(2,1)} %param.24) | copy-start | bytes 43012
  118.4 34.6 %copy-start = (bf16[16,7168]{1,0:T(8,128)(2,1)S(1)}, bf16[16,7168]{1,0:T(8,128)(2,1)}, u32[]{:S(2)}) copy-start(bf16[16,7168]{1,0:T(8,128)(2,1)} %get-tuple-element.8) | copy-start | bytes 688132
